TPU v7x, 32 devices: a whole 2x2x4 slice. The times are simulated.
32 devices in a mesh: blk: 8 (over y, x, core), col: 4 (over z).
Axes of the slice: x: 2, y: 2, z: 4, core: 2. Of those that a mesh axis runs over, the one named last changes fastest.
Arguments:
- features: bfloat16 [4096, 768], P(('blk', 'col')), may hold values from -6 to 6
- node_order: int32 [32, 128], P(('blk', 'col')), may hold values from 0 to 127, each once within a row
- weight: bfloat16 [768, 256], replicated, may hold values from -0.21875 to 0.21875
- cotangent: bfloat16 [4096, 256], P(('blk', 'col')), may hold values from -6 to 6
- tile_list: int32 [768, 2], P(('blk', 'col')), may hold values from -1 to 31, as said below
- tile_values: bfloat16 [768, 128, 128], P(('blk', 'col')), may hold values from -0.15625 to 0.15625
Outputs:
- hidden: bfloat16 [4096, 256], P(('blk', 'col'))
- x_grad: bfloat16 [4096, 768], P(('blk', 'col'))
- weight_grad: float32 [768, 256], replicated
Inputs may be any that keep to these rules, and one draw needn't show every extreme that they name: `tile_list`: slots held by one device come in groups of 3, group g taking tiles whose column block is among the 1 block that device (blk index g, the holder's col index) holds. A live slot's row block is among the 4 blocks of the holder's blk index; an empty slot has row block -1 and a valid column block. Every device has at least one full group.
All inputs are finite; a program needn't handle non-finite values.
Results may differ from a plain program's by a relative error of at most 0.0075.
Values may be sent and summed in bfloat16 or wider, within the bound.
A program may use at most 128 MiB of HBM per device.

v0:
```python
import jax
import jax.numpy as jnp
from jax import lax
from jax.sharding import PartitionSpec as P

SLOTS = 3


def shifted(value, axis, steps):
    count = lax.axis_size(axis)
    pairs = [(source, (source + steps) % count) for source in range(count)]
    return lax.ppermute(value, axis, pairs)


def gelu_tanh(values):
    return jax.nn.gelu(values, approximate=True)


def gelu_backward(values, upstream):
    _, pull = jax.vjp(gelu_tanh, values)
    return pull(upstream.astype(jnp.float32))[0].astype(jnp.bfloat16)


def per_device(features, node_order, weight, cotangent, tile_list, tile_values):
    tile_size = tile_values.shape[1]
    hidden_width = weight.shape[1]
    in_width = weight.shape[0]
    own_blocks = node_order.shape[0]
    col_count = lax.axis_size("col")
    blk_count = lax.axis_size("blk")
    range_blocks = own_blocks * col_count
    own_rows = own_blocks * tile_size
    lanes = jnp.arange(tile_size, dtype=jnp.int32)
    order_onehot = (node_order[:, :, None] == lanes[None, None, :]).astype(jnp.bfloat16)
    feature_blocks = features.reshape(own_blocks, tile_size, in_width)
    reordered = jnp.einsum(
        "qik,qkf->qif", order_onehot, feature_blocks, preferred_element_type=jnp.float32
    )
    reordered = reordered.astype(jnp.bfloat16).reshape(own_rows, in_width)
    panel = jnp.dot(reordered, weight, preferred_element_type=jnp.float32).astype(jnp.bfloat16)
    row_ids = tile_list[:, 0]
    col_ids = tile_list[:, 1]
    row_local = jnp.where(row_ids >= 0, row_ids % range_blocks, -1)
    row_target = jnp.where(row_ids >= 0, row_ids % range_blocks, range_blocks)
    col_local = col_ids % own_blocks
    range_ids = jnp.arange(range_blocks, dtype=jnp.int32)
    row_select = (row_local[:, None] == range_ids[None, :]).astype(jnp.bfloat16)
    empty = jnp.zeros((range_blocks + 1, tile_size, hidden_width), jnp.float32)
    piece = lax.all_gather(panel, "blk", axis=0, tiled=True)
    group_count = piece.shape[0] // own_rows
    slot_count = group_count * SLOTS
    part_tiles = tile_values
    part_cols = col_local
    part_rows = row_target
    position = jnp.arange(slot_count, dtype=jnp.int32) // SLOTS * own_blocks + part_cols
    piece_blocks = piece.reshape(group_count * own_blocks, tile_size, hidden_width)
    picked = jnp.take(piece_blocks, position, axis=0)
    product = jnp.einsum("sij,sjf->sif", part_tiles, picked, preferred_element_type=jnp.float32)
    partial_value = empty.at[part_rows].add(product)
    partial_value = partial_value[:range_blocks].reshape(range_blocks * tile_size, hidden_width)
    own_agg = lax.psum_scatter(partial_value, "col", scatter_dimension=0, tiled=True)
    hidden = gelu_tanh(own_agg).astype(jnp.bfloat16)
    own_grad = gelu_backward(own_agg, cotangent)
    grad_range = lax.all_gather(own_grad, "col", axis=0, tiled=True)
    grad_blocks = grad_range.reshape(range_blocks, tile_size, hidden_width)

    def contribution(group, width):
        part_tiles = lax.dynamic_slice_in_dim(tile_values, group * SLOTS, SLOTS, 0)
        part_rows = lax.dynamic_slice_in_dim(row_select, group * SLOTS, SLOTS, 0)
        part_cols = lax.dynamic_slice_in_dim(col_local, group * SLOTS, SLOTS, 0)
        grad_sel = jnp.einsum(
            "sr,rif->sif", part_rows, grad_blocks, preferred_element_type=jnp.float32
        )
        grad_sel = grad_sel.astype(jnp.bfloat16)
        product = jnp.einsum(
            "sij,sif->sjf", part_tiles, grad_sel, preferred_element_type=jnp.float32
        )
        placed = jnp.zeros((own_blocks, tile_size, width), jnp.float32).at[part_cols].add(product)
        return placed.reshape(own_rows, width)

    blk_here = lax.axis_index("blk")
    grad_total = contribution(jnp.mod(blk_here - 1, blk_count), hidden_width)

    def cycle_single(turn, carried):
        carried = shifted(carried, "blk", 1)
        return carried + contribution(jnp.mod(blk_here - turn - 1, blk_count), hidden_width)

    grad_total = lax.fori_loop(1, blk_count, cycle_single, grad_total)
    panel_grad = grad_total.astype(jnp.bfloat16)
    weight_term = lax.dot_general(
        reordered, panel_grad, (((0,), (0,)), ((), ())), preferred_element_type=jnp.float32
    )
    node_total = own_rows * col_count * blk_count
    weight_grad = lax.psum(weight_term, ("blk", "col")) * node_total ** (-0.5)
    row_grad = lax.dot_general(
        panel_grad, weight, (((1,), (1,)), ((), ())), preferred_element_type=jnp.float32
    )
    row_grad = row_grad.astype(jnp.bfloat16).reshape(own_blocks, tile_size, in_width)
    x_grad = jnp.einsum("qik,qif->qkf", order_onehot, row_grad, preferred_element_type=jnp.float32)
    x_grad = x_grad.astype(jnp.bfloat16).reshape(own_rows, in_width)
    return (hidden, x_grad, weight_grad)


def solution(mesh):
    in_specs = (
        P(("blk", "col"), None),
        P(("blk", "col"), None),
        P(),
        P(("blk", "col"), None),
        P(("blk", "col"), None),
        P(("blk", "col"), None, None),
    )
    out_specs = (P(("blk", "col"), None), P(("blk", "col"), None), P())
    return jax.shard_map(
        per_device, mesh=mesh, in_specs=in_specs, out_specs=out_specs, check_vma=False
    )
```

profile of v0, /device:TPU:1, one launch (start us, length us, event | category | flops | bytes accessed | tf_op | source)
XLA Modules:
  0.0 246.3 jit_solution(16476207447056284501)
XLA Ops:
  7.2 0.0 copy-start
  7.2 0.0 reduce-scatter.2.cloned.1.call-start
  7.3 1.2 convolution_convert_fusion.2
  8.5 0.0 copy-start.2
  8.5 0.7 copy-done.2
  9.2 0.2 convolution_convert_fusion.3
  9.4 11.2 %all_gather.6 = bf16[1024,256]{1,0:T(8,128)(2,1)S(1)} all-gather(bf16[128,256]{1,0:T(8,128)(2,1)S(1)} %convolution_convert_fusion.3), channel_id=1, replica_groups=mesh['blk'=8,'col'=4] {'blk'}, dimensions={0}, use_global_device_ids=true | all-gather | bytes 589824 | tf_op jit(solution)/shard_map/all_gather | solution.py:49
  20.6 1.9 gather_fusion
  22.5 2.3 convolution_bitcast_fusion
  24.8 0.0 copy-start.6
  24.8 2.3 copy.13
  27.2 6.1 %scatter_fusion.1 = f32[5,128,256]{2,1,0:T(8,128)S(1)} fusion(f32[5,128,256]{2,1,0:T(8,128)S(1)} %broadcast_in_dim.30, s32[24]{0:T(128)S(1)} %fusion.38, f32[24,128,256]{2,1,0:T(8,128)} %copy.13), kind=kCustom, calls=%fused_computation.2 | custom fusion | flops 786432 | bytes 9437280 | tf_op jit(solution)/shard_map/scatter-add | solution.py:59
  33.3 0.8 slice.11
  34.2 0.0 reduce-scatter.2.cloned.1.call-update
  34.2 0.0 all-reduce.2.cloned.1.call-start
  34.3 0.4 copy-done.1
  34.6 0.4 copy.14
  35.0 18.8 %reduce-scatter.2.cloned.1.call-done = f32[128,256]{1,0:T(8,128)} async-done(((f32[512,256]{1,0:T(8,128)}), f32[128,256]{1,0:T(8,128)}) %reduce-scatter.2.cloned.1.call-update) | async-done | bytes 131088 | tf_op jit(solution)/shard_map/reduce_scatter | solution.py:61
  53.9 1.6 fusion.16
  55.5 11.3 %all_gather.7 = bf16[512,256]{1,0:T(8,128)(2,1)S(1)} all-gather(bf16[128,256]{1,0:T(8,128)(2,1)S(1)} %get-tuple-element.204), channel_id=1, replica_groups=mesh['blk'=8,'col'=4] {'col'}, dimensions={0}, use_global_device_ids=true | all-gather | bytes 327680 | tf_op jit(solution)/shard_map/all_gather | solution.py:64
  66.8 0.4 fusion.11
  67.2 0.2 fusion.13
  67.5 0.9 scatter_fusion.2
  68.3 38.7 %while.15 = (s32[]{:T(128)}, f32[128,256]{1,0:T(8,128)S(1)}, s32[]{:T(128)}, bf16[24,128,128]{1,2,0:T(8,128)(2,1)S(1)}, bf16[24,4]{0,1:T(4,128)(2,1)S(1)}, /*ind...) while((s32[]{:T(128)}, f32[128,256]{1,0:T(8,128)S(1)}, ...), condition=%wide.region_5.6_spmd, body=%wide.region_3.5_spmd.sunk | while | flops 26083348 | bytes 3441224 | solution.py:88
  68.3 6.5 %collective-permute-start = (f32[128,256]{1,0:T(8,128)S(1)}, f32[128,256]{1,0:T(8,128)S(1)}, u32[]{:S(2)}, u32[]{:S(2)}) collective-permute-start(f32[128,256]{1,0:T(8,128)S(1)} %get-tuple-element.260), channel_id=1, source_target_pairs={{0,4},{4,8},{8,12},{12,16},{16,20},{20,24},{24,28},{28,0},{1,5},{5... | collective-permute-start | bytes 393224 | tf_op jit(solution)/shard_map/while/body/eval_jaxpr/ppermute | solution.py:12
  74.8 0.4 fusion.55
  75.3 0.2 fusion.56
  75.5 0.9 scatter_fusion
  76.4 0.4 collective-permute-done
  76.8 2.5 %collective-permute-start = (f32[128,256]{1,0:T(8,128)S(1)}, f32[128,256]{1,0:T(8,128)S(1)}, u32[]{:S(2)}, u32[]{:S(2)}) collective-permute-start(f32[128,256]{1,0:T(8,128)S(1)} %get-tuple-element.260), channel_id=1, source_target_pairs={{0,4},{4,8},{8,12},{12,16},{16,20},{20,24},{24,28},{28,0},{1,5},{5... | collective-permute-start | bytes 393224 | tf_op jit(solution)/shard_map/while/body/eval_jaxpr/ppermute | solution.py:12
  79.3 0.4 fusion.55
  79.8 0.2 fusion.56
  80.0 0.9 scatter_fusion
  80.8 0.4 collective-permute-done
  81.3 2.5 %collective-permute-start = (f32[128,256]{1,0:T(8,128)S(1)}, f32[128,256]{1,0:T(8,128)S(1)}, u32[]{:S(2)}, u32[]{:S(2)}) collective-permute-start(f32[128,256]{1,0:T(8,128)S(1)} %get-tuple-element.260), channel_id=1, source_target_pairs={{0,4},{4,8},{8,12},{12,16},{16,20},{20,24},{24,28},{28,0},{1,5},{5... | collective-permute-start | bytes 393224 | tf_op jit(solution)/shard_map/while/body/eval_jaxpr/ppermute | solution.py:12
  83.8 0.4 fusion.55
  84.2 0.2 fusion.56
  84.5 0.9 scatter_fusion
  85.3 0.4 collective-permute-done
  85.8 2.5 %collective-permute-start = (f32[128,256]{1,0:T(8,128)S(1)}, f32[128,256]{1,0:T(8,128)S(1)}, u32[]{:S(2)}, u32[]{:S(2)}) collective-permute-start(f32[128,256]{1,0:T(8,128)S(1)} %get-tuple-element.260), channel_id=1, source_target_pairs={{0,4},{4,8},{8,12},{12,16},{16,20},{20,24},{24,28},{28,0},{1,5},{5... | collective-permute-start | bytes 393224 | tf_op jit(solution)/shard_map/while/body/eval_jaxpr/ppermute | solution.py:12
  88.3 0.4 fusion.55
  88.7 0.2 fusion.56
  88.9 0.9 scatter_fusion
  89.8 1.1 collective-permute-done
  90.9 1.9 collective-permute-start
  92.8 0.4 fusion.55
  93.2 0.2 fusion.56
  93.4 0.9 scatter_fusion
  94.3 1.9 collective-permute-done
  96.3 1.0 collective-permute-start
  97.2 0.4 fusion.55
  97.7 0.2 fusion.56
  97.9 0.9 scatter_fusion
  98.8 2.8 %collective-permute-done = f32[128,256]{1,0:T(8,128)S(1)} collective-permute-done((f32[128,256]{1,0:T(8,128)S(1)}, f32[128,256]{1,0:T(8,128)S(1)}, u32[]{:S(2)}, u32[]{:S(2)}) %collective-permute-start) | collective-permute-done | bytes 131104 | tf_op jit(solution)/shard_map/while/body/eval_jaxpr/ppermute | solution.py:12
  101.6 0.1 collective-permute-start
  101.7 0.4 fusion.55
  102.1 0.2 fusion.56
  102.4 0.9 scatter_fusion
  103.2 3.7 %collective-permute-done = f32[128,256]{1,0:T(8,128)S(1)} collective-permute-done((f32[128,256]{1,0:T(8,128)S(1)}, f32[128,256]{1,0:T(8,128)S(1)}, u32[]{:S(2)}, u32[]{:S(2)}) %collective-permute-start) | collective-permute-done | bytes 131104 | tf_op jit(solution)/shard_map/while/body/eval_jaxpr/ppermute | solution.py:12
  107.0 1.2 fusion.25
  108.2 0.0 all-reduce.2.cloned.1.call-update
  108.2 1.1 convolution_convert_fusion
  109.3 128.1 %all-reduce.2.cloned.1.call-done = f32[768,256]{1,0:T(8,128)} async-done(((f32[768,256]{1,0:T(8,128)}), f32[768,256]{1,0:T(8,128)}) %all-reduce.2.cloned.1.call-update) | async-done | bytes 786448 | tf_op jit(solution)/shard_map/psum | solution.py:94
  237.4 2.1 broadcast_multiply_fusion
  (39 shorter events, 0.4 us)
Async XLA Ops:
  7.2 2.0 copy-start
  7.2 46.7 %reduce-scatter.2.cloned.1.call-start = ((), (), s32[]{:S(2)}) async-start(), calls=%async_computation.1 | async-start | bytes 655360 | tf_op jit(solution)/shard_map/reduce_scatter | solution.py:61
  8.5 0.7 copy-start.2
  24.8 2.4 copy-start.6
  33.3 1.3 copy-start.1
  33.3 20.6 %copy-start.4 = (bf16[128,256]{1,0:T(8,128)(2,1)S(1)}, bf16[128,256]{1,0:T(8,128)(2,1)}, u32[]{:S(2)}) copy-start(bf16[128,256]{1,0:T(8,128)(2,1)} %param.11) | copy-start | bytes 196612
  34.2 203.3 %all-reduce.2.cloned.1.call-start = ((), (), s32[]{:S(2)}) async-start(), calls=%async_computation.2 | async-start | bytes 1572864 | tf_op jit(solution)/shard_map/psum | solution.py:94
  68.3 38.7 %copy-start.3 = (bf16[128,768]{1,0:T(8,128)(2,1)S(1)}, bf16[128,768]{1,0:T(8,128)(2,1)}, u32[]{:S(2)}) copy-start(bf16[128,768]{1,0:T(8,128)(2,1)} %copy-done.2) | copy-start | bytes 589828
  68.3 8.5 %collective-permute-start = (f32[128,256]{1,0:T(8,128)S(1)}, f32[128,256]{1,0:T(8,128)S(1)}, u32[]{:S(2)}, u32[]{:S(2)}) collective-permute-start(f32[128,256]{1,0:T(8,128)S(1)} %get-tuple-element.260), channel_id=1, source_target_pairs={{0,4},{4,8},{8,12},{12,16},{16,20},{20,24},{24,28},{28,0},{1,5},{5... | collective-permute-start | bytes 393224 | tf_op jit(solution)/shard_map/while/body/eval_jaxpr/ppermute | solution.py:12
  76.8 4.4 %collective-permute-start = (f32[128,256]{1,0:T(8,128)S(1)}, f32[128,256]{1,0:T(8,128)S(1)}, u32[]{:S(2)}, u32[]{:S(2)}) collective-permute-start(f32[128,256]{1,0:T(8,128)S(1)} %get-tuple-element.260), channel_id=1, source_target_pairs={{0,4},{4,8},{8,12},{12,16},{16,20},{20,24},{24,28},{28,0},{1,5},{5... | collective-permute-start | bytes 393224 | tf_op jit(solution)/shard_map/while/body/eval_jaxpr/ppermute | solution.py:12
  81.3 4.4 %collective-permute-start = (f32[128,256]{1,0:T(8,128)S(1)}, f32[128,256]{1,0:T(8,128)S(1)}, u32[]{:S(2)}, u32[]{:S(2)}) collective-permute-start(f32[128,256]{1,0:T(8,128)S(1)} %get-tuple-element.260), channel_id=1, source_target_pairs={{0,4},{4,8},{8,12},{12,16},{16,20},{20,24},{24,28},{28,0},{1,5},{5... | collective-permute-start | bytes 393224 | tf_op jit(solution)/shard_map/while/body/eval_jaxpr/ppermute | solution.py:12
  85.8 5.1 %collective-permute-start = (f32[128,256]{1,0:T(8,128)S(1)}, f32[128,256]{1,0:T(8,128)S(1)}, u32[]{:S(2)}, u32[]{:S(2)}) collective-permute-start(f32[128,256]{1,0:T(8,128)S(1)} %get-tuple-element.260), channel_id=1, source_target_pairs={{0,4},{4,8},{8,12},{12,16},{16,20},{20,24},{24,28},{28,0},{1,5},{5... | collective-permute-start | bytes 393224 | tf_op jit(solution)/shard_map/while/body/eval_jaxpr/ppermute | solution.py:12
  90.9 5.3 %collective-permute-start = (f32[128,256]{1,0:T(8,128)S(1)}, f32[128,256]{1,0:T(8,128)S(1)}, u32[]{:S(2)}, u32[]{:S(2)}) collective-permute-start(f32[128,256]{1,0:T(8,128)S(1)} %get-tuple-element.260), channel_id=1, source_target_pairs={{0,4},{4,8},{8,12},{12,16},{16,20},{20,24},{24,28},{28,0},{1,5},{5... | collective-permute-start | bytes 393224 | tf_op jit(solution)/shard_map/while/body/eval_jaxpr/ppermute | solution.py:12
  96.3 5.3 %collective-permute-start = (f32[128,256]{1,0:T(8,128)S(1)}, f32[128,256]{1,0:T(8,128)S(1)}, u32[]{:S(2)}, u32[]{:S(2)}) collective-permute-start(f32[128,256]{1,0:T(8,128)S(1)} %get-tuple-element.260), channel_id=1, source_target_pairs={{0,4},{4,8},{8,12},{12,16},{16,20},{20,24},{24,28},{28,0},{1,5},{5... | collective-permute-start | bytes 393224 | tf_op jit(solution)/shard_map/while/body/eval_jaxpr/ppermute | solution.py:12
  101.6 5.3 %collective-permute-start = (f32[128,256]{1,0:T(8,128)S(1)}, f32[128,256]{1,0:T(8,128)S(1)}, u32[]{:S(2)}, u32[]{:S(2)}) collective-permute-start(f32[128,256]{1,0:T(8,128)S(1)} %get-tuple-element.260), channel_id=1, source_target_pairs={{0,4},{4,8},{8,12},{12,16},{16,20},{20,24},{24,28},{28,0},{1,5},{5... | collective-permute-start | bytes 393224 | tf_op jit(solution)/shard_map/while/body/eval_jaxpr/ppermute | solution.py:12
  107.0 1.2 copy-start.5
Sparse Core Ops, SparseCore 0:
  34.3 19.5 reduce-scatter.1
  108.3 129.0 all-reduce.1
where the time goes:
time: 248 us; the launch traced here: 246 us
  waiting for transfers between devices  158 us (64%)
  blocking collectives  22.5 us (9%)
  starting transfers between devices  17 us (7%)
  other arithmetic  16.8 us (7%)
  between operations  14.3 us (6%)
  matrix products  10.9 us (4%)
  local copies, waits for them, and re-layouts  6.67 us (3%)
    psum x1, waiting for transfers between devices, per_device(): weight_grad = lax.psum(weight_term, ('blk', 'col')) * node_total ** (-0.5)  128 us
    reduce_scatter x1, waiting for transfers between devices, per_device(): lax.psum_scatter(partial_value, 'col', scatter_dimension=0, tiled=True)  18.8 us
    ppermute x7, starting transfers between devices, shifted(): return lax.ppermute(value, axis, pairs)  16.9 us
    all_gather x1, blocking collectives, per_device(): grad_range = lax.all_gather(own_grad, 'col', axis=0, tiled=True)  11.3 us
    all_gather x1, blocking collectives, per_device(): piece = lax.all_gather(panel, 'blk', axis=0, tiled=True)  11.2 us
    ppermute x7, waiting for transfers between devices, shifted(): return lax.ppermute(value, axis, pairs)  10.9 us
    scatter-add x8, other arithmetic, contribution(): jnp.zeros((own_blocks, tile_size, width), jnp.float32).at[part_cols]  6.83 us
    scatter-add x1, other arithmetic, per_device(): partial_value = empty.at[part_rows].add(product)  6.05 us
  transfers between devices with their start and end apart: 9, of which 9 were waited for; matrix products, arithmetic and copies ran while one was open for 5% of the time, Pallas kernels for 0%

commit v1 on v0

v1 whole, which is shorter than its diff:
```python
import functools

import jax
import jax.numpy as jnp
from jax import lax
from jax.experimental import pallas as pl
from jax.experimental.pallas import tpu as pltpu
from jax.sharding import PartitionSpec as P

SLOTS = 3
MESH = pl.DeviceIdType.MESH
F32 = jnp.float32
BF16 = jnp.bfloat16


def dot(a, b):
    return jnp.dot(a, b, preferred_element_type=F32)


def kernel(
    dims, scale,
    feat_h, order_h, weight_h, cot_h, list_ref, tiles_h,
    hidden_ref, xgrad_ref, wgrad_ref,
    feat, order, weight, cot, tiles,
    adj, adj_t, feat_t, panels, part, part16, agg_in, grads, pg_part, pg16,
    pair_in, chip_out, chip_in, dw_part, dw16, dw_pair, dw_sum, dw_sum16, dw_chip,
    dw_col, dw_all,
    in_sem, ag_s, ag_r, rc_s, rc_r, gc_s, gc_r, pp_s, pp_r, pc_s, pc_r,
    dp_s, dp_r, dc_s, dc_r, dz_s, dz_r, dg_s, dg_r, dh_s, dh_r, di_s, di_r,
):
    n_blk, n_col, tile, fin, hid = dims
    n_chip = n_blk // 2
    half = hid // 2
    b = lax.axis_index("blk")
    c = lax.axis_index("col")
    chip = b // 2
    core = b % 2
    sib = b + 1 - 2 * core
    sends = []

    def rows(i, n=tile):
        return pl.ds(pl.multiple_of(i * n, n), n)

    def send(src, dst, s_sem, r_sem, blk, col):
        copy = pltpu.make_async_remote_copy(
            src_ref=src, dst_ref=dst, send_sem=s_sem, recv_sem=r_sem,
            device_id=(blk, col), device_id_type=MESH,
        )
        copy.start()
        sends.append(copy)

    def arrive(dst, s_sem, r_sem):
        pltpu.make_async_remote_copy(
            src_ref=dst, dst_ref=dst, send_sem=s_sem, recv_sem=r_sem,
            device_id=(sib, c), device_id_type=MESH,
        ).wait_recv()

    def other_chips():
        return [(k, (chip + k) % n_chip, (chip + n_chip - k) % n_chip) for k in range(1, n_chip)]

    def other_cols():
        return [(k, (c + k) % n_col, (c + n_col - k) % n_col) for k in range(1, n_col)]

    loads = []
    for i, (src, dst) in enumerate(
        ((feat_h, feat), (weight_h, weight), (order_h, order), (tiles_h, tiles), (cot_h, cot))
    ):
        copy = pltpu.make_async_copy(src, dst, in_sem.at[i])
        copy.start()
        loads.append(copy)

    barrier = pltpu.get_barrier_semaphore()
    peers = [(sib, c)]
    peers += [(2 * to + core, c) for _, to, _ in other_chips()]
    peers += [(b, to) for _, to, _ in other_cols()]
    for peer in peers:
        pl.semaphore_signal(barrier, inc=1, device_id=peer, device_id_type=MESH)

    loads[0].wait()
    loads[1].wait()
    loads[2].wait()
    place = (
        lax.broadcasted_iota(jnp.int32, (tile, tile), 0) == order[...]
    ).astype(F32).astype(BF16)
    mixed = dot(feat[...], weight[...]).astype(BF16)
    panel = lax.dot_general(
        place, mixed, (((0,), (0,)), ((), ())), preferred_element_type=F32
    ).astype(BF16)
    panels[rows(b), :] = panel
    pl.semaphore_wait(barrier, len(peers))

    for k, to, _ in other_chips():
        send(panels.at[rows(b)], panels.at[rows(b)], ag_s.at[k], ag_r.at[b], 2 * to + core, c)
    send(panels.at[rows(b)], panels.at[rows(b)], ag_s.at[0], ag_r.at[b], sib, c)

    loads[3].wait()

    def build(g, _):
        held = [tiles[g * SLOTS + s] for s in range(SLOTS)]
        ids = [list_ref[g * SLOTS + s, 0] - b * n_col for s in range(SLOTS)]
        for r in range(n_col):
            block = jnp.zeros((tile, tile), BF16)
            for t, i in zip(held, ids):
                block = block + jnp.where(i == r, t, jnp.zeros_like(t))
            adj[r * tile:(r + 1) * tile, rows(g)] = block
        return 0

    lax.fori_loop(0, n_blk, build, 0)

    for k, _, src in other_chips():
        at = panels.at[rows(2 * src + core)]
        arrive(at, ag_s.at[k], ag_r.at[2 * src + core])
        send(at, at, ag_s.at[n_chip + k], ag_r.at[2 * src + core], sib, c)
    arrive(panels.at[rows(sib)], ag_s.at[0], ag_r.at[sib])
    for k, _, src in other_chips():
        at = 2 * src + 1 - core
        arrive(panels.at[rows(at)], ag_s.at[k], ag_r.at[at])

    step = 4 * tile if n_col % 4 == 0 else tile

    def forward(i, _):
        got = dot(adj[rows(i, step), :], panels[...])
        part[rows(i, step), :] = got
        part16[rows(i, step), :] = got.astype(BF16)
        return 0

    lax.fori_loop(0, n_col * tile // step, forward, 0)
    for k, to, _ in other_cols():
        send(part16.at[rows(to)], agg_in.at[rows(c)], rc_s.at[k], rc_r.at[c], b, to)

    def turn(g, _):
        for r in range(n_col):
            adj_t[rows(g), r * tile:(r + 1) * tile] = (
                adj[r * tile:(r + 1) * tile, rows(g)].T
            )
        return 0

    lax.fori_loop(0, n_blk, turn, 0)
    for i in range(fin // tile):
        feat_t[i * tile:(i + 1) * tile, :] = feat[:, i * tile:(i + 1) * tile].T
    loads[4].wait()

    agg = part[rows(c), :]
    for k, _, src in other_cols():
        arrive(agg_in.at[rows(src)], rc_s.at[k], rc_r.at[src])
        agg = agg + agg_in[rows(src), :].astype(F32)

    root = 0.7978845608028654
    inner = root * (agg + 0.044715 * agg * agg * agg)
    th = jnp.tanh(inner)
    slope = 0.5 * (1.0 + th) + 0.5 * agg * (1.0 - th * th) * (
        root * (1.0 + 3 * 0.044715 * agg * agg)
    )
    grads[rows(c), :] = (cot[...].astype(F32) * slope).astype(BF16)
    for k, to, _ in other_cols():
        send(grads.at[rows(c)], grads.at[rows(c)], gc_s.at[k], gc_r.at[c], b, to)
    hidden_ref[...] = (0.5 * agg * (1.0 + th)).astype(BF16)
    for k, _, src in other_cols():
        arrive(grads.at[rows(src)], gc_s.at[k], gc_r.at[src])

    bstep = 4 * tile if n_blk % 4 == 0 else tile

    def backward(i, _):
        got = dot(adj_t[rows(i, bstep), :], grads[...])
        pg_part[rows(i, bstep), :] = got
        pg16[rows(i, bstep), :] = got.astype(BF16)
        return 0

    lax.fori_loop(0, n_blk * tile // bstep, backward, 0)
    order_out = other_chips() + [(0, chip, chip)]
    for k, to, _ in order_out:
        send(
            pg16.at[rows(2 * to + 1 - core)], pair_in.at[rows(to)],
            pp_s.at[k], pp_r.at[to], sib, c,
        )
    for k, to, _ in order_out[:-1]:
        arrive(pair_in.at[rows(to)], pp_s.at[k], pp_r.at[to])
        both = pg_part[rows(2 * to + core), :] + pair_in[rows(to), :].astype(F32)
        chip_out[rows(to), :] = both.astype(BF16)
        send(
            chip_out.at[rows(to)], chip_in.at[rows(chip)],
            pc_s.at[k], pc_r.at[chip], 2 * to + core, c,
        )
    arrive(pair_in.at[rows(chip)], pp_s.at[0], pp_r.at[chip])
    total = pg_part[rows(b), :] + pair_in[rows(chip), :].astype(F32)
    for k, _, src in other_chips():
        arrive(chip_in.at[rows(src)], pc_s.at[k], pc_r.at[src])
        total = total + chip_in[rows(src), :].astype(F32)
    back = dot(place, total.astype(BF16)).astype(BF16)

    term = dot(feat_t[...], back)
    dw_part[0] = term[:, :half]
    dw_part[1] = term[:, half:]
    dw16[0] = term[:, :half].astype(BF16)
    dw16[1] = term[:, half:].astype(BF16)
    send(dw16.at[1 - core], dw_pair, dp_s.at[0], dp_r.at[0], sib, c)
    xgrad_ref[...] = lax.dot_general(
        back, weight[...], (((1,), (1,)), ((), ())), preferred_element_type=F32
    ).astype(BF16)
    arrive(dw_pair, dp_s.at[0], dp_r.at[0])
    both = dw_part[core] + dw_pair[...].astype(F32)
    dw_sum[...] = both
    dw_sum16[...] = both.astype(BF16)
    r1 = fin // n_chip
    for k, to, _ in other_chips():
        send(
            dw_sum16.at[rows(to, r1)], dw_chip.at[rows(chip, r1)],
            dc_s.at[k], dc_r.at[chip], 2 * to + core, c,
        )
    piece = dw_sum[rows(chip, r1), :]
    for k, _, src in other_chips():
        arrive(dw_chip.at[rows(src, r1)], dc_s.at[k], dc_r.at[src])
        piece = piece + dw_chip[rows(src, r1), :].astype(F32)
    dw_sum[0:r1, :] = piece
    dw_sum16[rows(chip, r1), :] = piece.astype(BF16)
    if r1 % (16 * n_col) == 0:
        r2 = r1 // n_col
        for k, to, _ in other_cols():
            send(
                dw_sum16.at[rows(chip * n_col + to, r2)], dw_col.at[rows(c, r2)],
                dz_s.at[k], dz_r.at[c], b, to,
            )
        piece = dw_sum[rows(c, r2), :]
        for k, _, src in other_cols():
            arrive(dw_col.at[rows(src, r2)], dz_s.at[k], dz_r.at[src])
            piece = piece + dw_col[rows(src, r2), :].astype(F32)
        mine = chip * n_col + c
        dw_all[core, rows(mine, r2), :] = piece.astype(BF16)
        for k, to, _ in other_cols():
            at = dw_all.at[core, rows(mine, r2)]
            send(at, at, dg_s.at[k], dg_r.at[c], b, to)
        for k, _, src in other_cols():
            at = dw_all.at[core, rows(chip * n_col + src, r2)]
            arrive(at, dg_s.at[k], dg_r.at[src])
    else:
        dw_col[rows(c, r1), :] = piece.astype(BF16)
        for k, to, _ in other_cols():
            at = dw_col.at[rows(c, r1)]
            send(at, at, dz_s.at[k], dz_r.at[c], b, to)
        for k, _, src in other_cols():
            arrive(dw_col.at[rows(src, r1)], dz_s.at[k], dz_r.at[src])
        piece = dw_col[0:r1, :].astype(F32)
        for i in range(1, n_col):
            piece = piece + dw_col[i * r1:(i + 1) * r1, :].astype(F32)
        dw_all[core, rows(chip, r1), :] = piece.astype(BF16)
    at = dw_all.at[core, rows(chip, r1)]
    for k, to, _ in other_chips():
        send(at, at, dh_s.at[k], dh_r.at[chip], 2 * to + core, c)
    send(at, at, di_s.at[0], di_r.at[chip], sib, c)
    for k, _, src in other_chips():
        at = dw_all.at[core, rows(src, r1)]
        arrive(at, dh_s.at[k], dh_r.at[src])
        send(at, at, di_s.at[k], di_r.at[src], sib, c)
    for k, _, src in [(0, chip, chip)] + other_chips():
        arrive(dw_all.at[1 - core, rows(src, r1)], di_s.at[k], di_r.at[src])
    wgrad_ref[:, :half] = dw_all[0].astype(F32) * scale
    wgrad_ref[:, half:] = dw_all[1].astype(F32) * scale
    for copy in sends:
        copy.wait_send()


def per_device(features, node_order, weight, cotangent, tile_list, tile_values):
    n_blk, n_col = lax.axis_size("blk"), lax.axis_size("col")
    slots, tile, _ = tile_values.shape
    fin, hid = weight.shape
    n_chip = n_blk // 2
    scale = float(n_blk * n_col * tile) ** -0.5
    r1 = fin // n_chip
    dma = lambda n: pltpu.SemaphoreType.DMA((n,))
    vmem = pltpu.VMEM
    scratch = [
        vmem((tile, fin), BF16), vmem((1, tile), jnp.int32), vmem((fin, hid), BF16),
        vmem((tile, hid), BF16), vmem((slots, tile, tile), BF16),
        vmem((n_col * tile, n_blk * tile), BF16), vmem((n_blk * tile, n_col * tile), BF16),
        vmem((fin, tile), BF16), vmem((n_blk * tile, hid), BF16),
        vmem((n_col * tile, hid), F32), vmem((n_col * tile, hid), BF16),
        vmem((n_col * tile, hid), BF16), vmem((n_col * tile, hid), BF16),
        vmem((n_blk * tile, hid), F32), vmem((n_blk * tile, hid), BF16),
        vmem((n_chip * tile, hid), BF16), vmem((n_chip * tile, hid), BF16),
        vmem((n_chip * tile, hid), BF16),
        vmem((2, fin, hid // 2), F32), vmem((2, fin, hid // 2), BF16),
        vmem((fin, hid // 2), BF16), vmem((fin, hid // 2), F32),
        vmem((fin, hid // 2), BF16), vmem((fin, hid // 2), BF16),
        vmem((n_col * r1, hid // 2), BF16), vmem((2, fin, hid // 2), BF16),
        dma(5), dma(2 * n_chip), dma(n_blk), dma(n_col), dma(n_col), dma(n_col), dma(n_col),
        dma(n_chip), dma(n_chip), dma(n_chip), dma(n_chip),
        dma(1), dma(1), dma(n_chip), dma(n_chip), dma(n_col), dma(n_col),
        dma(n_col), dma(n_col), dma(n_chip), dma(n_chip), dma(n_chip), dma(n_chip),
    ]
    hbm = pl.BlockSpec(memory_space=pl.ANY)
    inside = pl.BlockSpec(memory_space=pltpu.VMEM)
    return pl.pallas_call(
        functools.partial(kernel, (n_blk, n_col, tile, fin, hid), scale),
        out_shape=(
            jax.ShapeDtypeStruct((tile, hid), BF16),
            jax.ShapeDtypeStruct((tile, fin), BF16),
            jax.ShapeDtypeStruct((fin, hid), F32),
        ),
        in_specs=[hbm, hbm, hbm, hbm, pl.BlockSpec(memory_space=pltpu.SMEM), hbm],
        out_specs=(inside, inside, inside),
        scratch_shapes=scratch,
        compiler_params=pltpu.CompilerParams(
            collective_id=0, has_side_effects=True, vmem_limit_bytes=60 * 1024 * 1024
        ),
        cost_estimate=pl.CostEstimate(
            flops=4 * slots * tile * tile * hid, bytes_accessed=4 * 1024 * 1024,
            transcendentals=tile * hid,
        ),
    )(features, node_order, weight, cotangent, tile_list, tile_values)


def solution(mesh):
    in_specs = (
        P(("blk", "col"), None),
        P(("blk", "col"), None),
        P(),
        P(("blk", "col"), None),
        P(("blk", "col"), None),
        P(("blk", "col"), None, None),
    )
    out_specs = (P(("blk", "col"), None), P(("blk", "col"), None), P())
    return jax.shard_map(
        per_device, mesh=mesh, in_specs=in_specs, out_specs=out_specs, check_vma=False
    )
```

time: 248 us -> 59.9 us (0.24)
  waiting for transfers between devices: 158 us -> 0 us
  Pallas kernels: 0 us -> 52.4 us
  blocking collectives: 22.5 us -> 0 us
  starting transfers between devices: 17 us -> 0 us
  other arithmetic: 16.8 us -> 0 us
  between operations: 14.3 us -> 0.64 us
  matrix products: 10.9 us -> 0 us
    psum x1 -> x0, waiting for transfers between devices: 128 us -> none  [per_device(): weight_grad = lax.psum(weight_term, ('blk', 'col')) * node_total ** (-0.5)]
    pallas_call x0 -> x1, Pallas kernels: none -> 52.4 us  [per_device(): pl.pallas_call(functools.partial(kernel, (n_blk, n_col, tile, fin, hid),...]
    all_gather x2 -> x0, blocking collectives: 22.5 us -> none  [the longest x1 11.3 us: per_device(): grad_range = lax.all_gather(own_grad, 'col', axis=0, tiled=True)]
    reduce_scatter x1 -> x0, waiting for transfers between devices: 18.8 us -> none  [per_device(): lax.psum_scatter(partial_value, 'col', scatter_dimension=0, tiled=True)]
    ppermute x7 -> x0, starting transfers between devices: 16.9 us -> none  [shifted(): return lax.ppermute(value, axis, pairs)]
    scatter-add x9 -> x0, other arithmetic: 12.9 us -> none  [the longest x8 6.83 us: contribution(): jnp.zeros((own_blocks, tile_size, width), jnp.float32).at[part_cols]]
    dot_general x21 -> x0, matrix products: 10.9 us -> none  [the longest x8 3.35 us: contribution(): jnp.einsum('sr,rif->sif', part_rows, grad_blocks, preferred_element_type=...]
    ppermute x7 -> x0, waiting for transfers between devices: 10.9 us -> none  [shifted(): return lax.ppermute(value, axis, pairs)]
  transfers between devices with their start and end apart: 9 -> 0, of which waited for: 9 -> 0; matrix products, arithmetic and copies ran while one was open for 5% -> 0% of each run, Pallas kernels for 0% -> 0%
where the time goes in v1:
time: 59.9 us; the launch traced here: 59.6 us
  Pallas kernels  52.4 us (87%)
  local copies, waits for them, and re-layouts  6.51 us (11%)
  between operations  0.64 us (1%)
    pallas_call x1, Pallas kernels, per_device(): pl.pallas_call(functools.partial(kernel, (n_blk, n_col, tile, fin, hid),...  52.4 us
    unnamed x4, local copies, waits for them, and re-layouts  6.51 us

profile of v1, /device:TPU:1, one launch (start us, length us, event | category | flops | bytes accessed | tf_op | source)
XLA Modules:
  0.0 59.6 jit_solution(2938340924279120300)
XLA Ops:
  0.6 1.4 %copy.9.list_ref = s32[24,2]{1,0:T(8,128)} copy(s32[24,2]{0,1:T(2,128)} %param.10) | data formatting | bytes 384 | tf_op args[4]
  2.0 52.4 %shard_map.85 = (bf16[128,256]{1,0:T(8,128)(2,1)}, bf16[128,768]{1,0:T(8,128)(2,1)}, f32[768,256]{1,0:T(8,128)}) custom-call(bf16[128,768]{1,0:T(8,128)(2,1)} %feat_h.1, s32[1,128]{1,0:T(1,128)} %order_h.1, bf16[768,256]{1,0:T(8,128)(2,1)} %weight_h.1, bf16[128,256]{1,0:T(8,128)(2,1)} %cot_h.1, s32[24,2]{1,0:T(8,128)} %copy.9.list_ref, ...), custom_call_target="tpu_custom_call" | custom-call | flops 402653184 | bytes 4194304 | tf_op jit(solution)/shard_map/pallas_call | solution.py:292
  54.4 1.5 %copy.13 = bf16[128,256]{1,0:T(8,128)(2,1)} copy(bf16[128,256]{1,0:T(8,128)(2,1)} %get-tuple-element.6) | data formatting | bytes 131072
  55.9 1.6 %copy.14 = bf16[128,768]{1,0:T(8,128)(2,1)} copy(bf16[128,768]{1,0:T(8,128)(2,1)} %get-tuple-element.7) | data formatting | bytes 393216
  57.5 2.1 %copy.15 = f32[768,256]{1,0:T(8,128)} copy(f32[768,256]{1,0:T(8,128)} %get-tuple-element.8) | data formatting | bytes 1572864

commit v2 on v1

v2 whole, which is shorter than its diff:
```python
import functools

import jax
import jax.numpy as jnp
from jax import lax
from jax.experimental import pallas as pl
from jax.experimental.pallas import tpu as pltpu
from jax.sharding import PartitionSpec as P

SLOTS = 3
MESH = pl.DeviceIdType.MESH
F32 = jnp.float32
BF16 = jnp.bfloat16


def dot(a, b):
    return jnp.dot(a, b, preferred_element_type=F32)


def kernel(
    dims,
    feat_h, order_h, weight_h, cot_h, list_ref, tiles_h,
    hidden_h, xgrad_h, wgrad_h,
    feat, order, weight, cot, tiles, hidden, xgrad,
    adj, adj_t, feat_t, feat_all, panels, part, part16, agg_in, grads, pg_part, pg16,
    pair_in, both16, chip_in, dw_sum, dw16, dw_chip, dw_mid, dw_mid16, dw_col, dw_all,
    in_sem, out_sem, ag_s, ag_r, rc_s, rc_r, gc_s, gc_r, pp_s, pp_r, pc_s, pc_r,
    fe_s, fe_r, dc_s, dc_r, dz_s, dz_r, dg_s, dg_r, dh_s, dh_r, di_s, di_r,
):
    n_blk, n_col, tile, fin, hid, r1, r2 = dims
    n_chip = n_blk // 2
    half = hid // 2
    fhalf = fin // 2
    b = lax.axis_index("blk")
    c = lax.axis_index("col")
    chip = b // 2
    core = b % 2
    sib = b + 1 - 2 * core
    sends = []

    def rows(i, n=tile):
        return pl.ds(pl.multiple_of(i * n, n), n)

    def send(src, dst, s_sem, r_sem, blk, col):
        copy = pltpu.make_async_remote_copy(
            src_ref=src, dst_ref=dst, send_sem=s_sem, recv_sem=r_sem,
            device_id=(blk, col), device_id_type=MESH,
        )
        copy.start()
        sends.append(copy)

    def arrive(dst, s_sem, r_sem):
        pltpu.make_async_remote_copy(
            src_ref=dst, dst_ref=dst, send_sem=s_sem, recv_sem=r_sem,
            device_id=(sib, c), device_id_type=MESH,
        ).wait_recv()

    chips = [(k, (chip + k) % n_chip, (chip + n_chip - k) % n_chip) for k in range(1, n_chip)]
    cols = [(k, (c + k) % n_col, (c + n_col - k) % n_col) for k in range(1, n_col)]

    loads = []
    for i, (src, dst) in enumerate(
        ((feat_h, feat), (weight_h, weight), (order_h, order), (tiles_h, tiles), (cot_h, cot))
    ):
        copy = pltpu.make_async_copy(src, dst, in_sem.at[i])
        copy.start()
        loads.append(copy)

    barrier = pltpu.get_barrier_semaphore()
    peers = [(sib, c)]
    peers += [(2 * to + core, c) for _, to, _ in chips]
    peers += [(2 * to + 1 - core, c) for _, to, _ in chips]
    peers += [(b, to) for _, to, _ in cols]
    for peer in peers:
        pl.semaphore_signal(barrier, inc=1, device_id=peer, device_id_type=MESH)

    loads[0].wait()
    loads[1].wait()
    loads[2].wait()
    place = (
        lax.broadcasted_iota(jnp.int32, (tile, tile), 0) == order[...]
    ).astype(F32).astype(BF16)
    mixed = dot(feat[...], weight[...]).astype(BF16)
    panel = lax.dot_general(
        place, mixed, (((0,), (0,)), ((), ())), preferred_element_type=F32
    ).astype(BF16)
    for h in range(2):
        panels[h, rows(b), :] = panel[:, h * half:(h + 1) * half]
    pl.semaphore_wait(barrier, len(peers))

    for h in range(2):
        at = panels.at[h, rows(b)]
        for k, to, _ in chips:
            send(at, at, ag_s.at[h, k], ag_r.at[h, b], 2 * to + core, c)
        send(at, at, ag_s.at[h, 0], ag_r.at[h, b], sib, c)

    loads[3].wait()

    def build(g, _):
        held = [tiles[g * SLOTS + s] for s in range(SLOTS)]
        ids = [list_ref[0, g * SLOTS + s] - b * n_col for s in range(SLOTS)]
        for r in range(n_col):
            block = jnp.zeros((tile, tile), BF16)
            for t, i in zip(held, ids):
                block = block + jnp.where(i == r, t, jnp.zeros_like(t))
            adj[r * tile:(r + 1) * tile, rows(g)] = block
        return 0

    lax.fori_loop(0, n_blk, build, 0)
    feat_t[...] = lax.dot_general(
        feat[...], place, (((0,), (0,)), ((), ())), preferred_element_type=F32
    ).astype(BF16)
    feat_all[:, rows(b)] = feat_t[rows(core, fhalf), :]

    step = 4 * tile if n_col % 4 == 0 else tile
    for h in range(2):
        for k, _, src in chips:
            at = panels.at[h, rows(2 * src + core)]
            arrive(at, ag_s.at[h, k], ag_r.at[h, 2 * src + core])
            send(at, at, ag_s.at[h, n_chip + k], ag_r.at[h, 2 * src + core], sib, c)
        arrive(panels.at[h, rows(sib)], ag_s.at[h, 0], ag_r.at[h, sib])
        for k, _, src in chips:
            at = 2 * src + 1 - core
            arrive(panels.at[h, rows(at)], ag_s.at[h, k], ag_r.at[h, at])

        def forward(i, _):
            got = dot(adj[rows(i, step), :], panels[h])
            part[h, rows(i, step), :] = got
            part16[h, rows(i, step), :] = got.astype(BF16)
            return 0

        lax.fori_loop(0, n_col * tile // step, forward, 0)
        for k, to, _ in cols:
            send(part16.at[h, rows(to)], agg_in.at[h, rows(c)], rc_s.at[h, k], rc_r.at[h, c], b, to)

    for k, to, _ in chips:
        for q in range(2):
            at = feat_all.at[:, rows(b)]
            send(feat_t.at[pl.ds(q * fhalf, fhalf)], at, fe_s.at[2 * k + q], fe_r.at[b], 2 * to + q, c)
    send(feat_t.at[rows(1 - core, fhalf)], feat_all.at[:, rows(b)], fe_s.at[0], fe_r.at[b], sib, c)

    def turn(g, _):
        for r in range(n_col):
            adj_t[rows(g), r * tile:(r + 1) * tile] = (
                adj[r * tile:(r + 1) * tile, rows(g)].T
            )
        return 0

    turned = adj_t.shape[0] > tile
    if turned:
        lax.fori_loop(0, n_blk, turn, 0)
    loads[4].wait()

    root = 0.7978845608028654
    for h in range(2):
        agg = part[h, rows(c), :]
        for k, _, src in cols:
            arrive(agg_in.at[h, rows(src)], rc_s.at[h, k], rc_r.at[h, src])
            agg = agg + agg_in[h, rows(src), :].astype(F32)
        inner = root * (agg + 0.044715 * agg * agg * agg)
        th = jnp.tanh(inner)
        slope = 0.5 * (1.0 + th) + 0.5 * agg * (1.0 - th * th) * (
            root * (1.0 + 3 * 0.044715 * agg * agg)
        )
        lanes = slice(h * half, (h + 1) * half)
        grads[h, rows(c), :] = (cot[:, lanes].astype(F32) * slope).astype(BF16)
        at = grads.at[h, rows(c)]
        for k, to, _ in cols:
            send(at, at, gc_s.at[h, k], gc_r.at[h, c], b, to)
        hidden[:, lanes] = (0.5 * agg * (1.0 + th)).astype(BF16)
    outs = [pltpu.make_async_copy(hidden, hidden_h, out_sem.at[0])]
    outs[0].start()

    bstep = 4 * tile if n_blk % 4 == 0 else tile
    for h in range(2):
        for k, _, src in cols:
            arrive(grads.at[h, rows(src)], gc_s.at[h, k], gc_r.at[h, src])

        def backward(i, _):
            if turned:
                got = dot(adj_t[rows(i, bstep), :], grads[h])
            else:
                got = lax.dot_general(
                    adj[:, rows(i, bstep)], grads[h], (((0,), (0,)), ((), ())),
                    preferred_element_type=F32,
                )
            pg_part[h, rows(i, bstep), :] = got
            pg16[h, rows(i, bstep), :] = got.astype(BF16)
            return 0

        lax.fori_loop(0, n_blk * tile // bstep, backward, 0)
        send(pg16.at[h], pair_in.at[h], pp_s.at[h], pp_r.at[h], sib, c)

    for k, _, src in chips:
        for q in range(2):
            at = feat_all.at[:, rows(2 * src + q)]
            arrive(at, fe_s.at[0], fe_r.at[2 * src + q])
    arrive(feat_all.at[:, rows(sib)], fe_s.at[0], fe_r.at[sib])

    for h in range(2):
        arrive(pair_in.at[h], pp_s.at[h], pp_r.at[h])
        both16[h] = (pg_part[h] + pair_in[h].astype(F32)).astype(BF16)
        term = dot(feat_all[...], both16[h])
        dw_sum[h, 0:fhalf, :] = term
        dw16[h, 0:fhalf, :] = term.astype(BF16)
        if n_chip * r1 > fhalf:
            rest = jnp.zeros((n_chip * r1 - fhalf, half), F32)
            dw_sum[h, fhalf:, :] = rest
            dw16[h, fhalf:, :] = rest.astype(BF16)
        for k, to, _ in chips:
            send(
                dw16.at[h, rows(to, r1)], dw_chip.at[h, rows(chip, r1)],
                dc_s.at[h, k], dc_r.at[h, chip], 2 * to + core, c,
            )
    for h in range(2):
        for k, to, _ in chips:
            send(
                both16.at[h, rows(2 * to + core)], chip_in.at[h, rows(chip)],
                pc_s.at[h, k], pc_r.at[h, chip], 2 * to + core, c,
            )
    for h in range(2):
        piece = dw_sum[h, rows(chip, r1), :]
        for k, _, src in chips:
            arrive(dw_chip.at[h, rows(src, r1)], dc_s.at[h, k], dc_r.at[h, src])
            piece = piece + dw_chip[h, rows(src, r1), :].astype(F32)
        dw_mid[h, 0:r1, :] = piece
        dw_mid16[h, 0:r1, :] = piece.astype(BF16)
        if n_col * r2 > r1:
            rest = jnp.zeros((n_col * r2 - r1, half), F32)
            dw_mid[h, r1:, :] = rest
            dw_mid16[h, r1:, :] = rest.astype(BF16)
        for k, to, _ in cols:
            send(
                dw_mid16.at[h, rows(to, r2)], dw_col.at[h, rows(c, r2)],
                dz_s.at[h, k], dz_r.at[h, c], b, to,
            )
    for h in range(2):
        piece = dw_mid[h, rows(c, r2), :]
        for k, _, src in cols:
            arrive(dw_col.at[h, rows(src, r2)], dz_s.at[h, k], dz_r.at[h, src])
            piece = piece + dw_col[h, rows(src, r2), :].astype(F32)
        dw_all[core, h, chip, rows(c, r2), :] = piece.astype(BF16)
        at = dw_all.at[core, h, chip, rows(c, r2)]
        for k, to, _ in cols:
            send(at, at, dg_s.at[h, k], dg_r.at[h, c], b, to)

    sums = []
    for h in range(2):
        total = pg_part[h, rows(b), :] + pair_in[h, rows(b), :].astype(F32)
        for k, _, src in chips:
            arrive(chip_in.at[h, rows(src)], pc_s.at[h, k], pc_r.at[h, src])
            total = total + chip_in[h, rows(src), :].astype(F32)
        sums.append(total.astype(BF16))
    back = dot(place, jnp.concatenate(sums, axis=1)).astype(BF16)
    xgrad[...] = lax.dot_general(
        back, weight[...], (((1,), (1,)), ((), ())), preferred_element_type=F32
    ).astype(BF16)
    outs.append(pltpu.make_async_copy(xgrad, xgrad_h, out_sem.at[1]))
    outs[1].start()

    for h in range(2):
        for k, _, src in cols:
            at = dw_all.at[core, h, chip, rows(src, r2)]
            arrive(at, dg_s.at[h, k], dg_r.at[h, src])
        at = dw_all.at[core, h, chip, pl.ds(0, r1)]
        for k, to, _ in chips:
            send(at, at, dh_s.at[h, k], dh_r.at[h, chip], 2 * to + core, c)
        send(at, at, di_s.at[h, 0], di_r.at[h, chip], sib, c)
    for h in range(2):
        for k, _, src in chips:
            at = dw_all.at[core, h, src, pl.ds(0, r1)]
            arrive(at, dh_s.at[h, k], dh_r.at[h, src])
            send(at, at, di_s.at[h, k], di_r.at[h, src], sib, c)
    for h in range(2):
        for k, _, src in [(0, chip, chip)] + chips:
            at = dw_all.at[1 - core, h, src, pl.ds(0, r1)]
            arrive(at, di_s.at[h, k], di_r.at[h, src])
    for copy in sends:
        copy.wait_send()
    outs.append(pltpu.make_async_copy(dw_all.at[:, :, :, pl.ds(0, r1)], wgrad_h, out_sem.at[2]))
    outs[2].start()
    for copy in outs:
        copy.wait()


def finish(scale, r1, hidden_in, xgrad_in, wgrad_in, hidden_ref, xgrad_ref, wgrad_ref):
    hidden_ref[...] = hidden_in[...]
    xgrad_ref[...] = xgrad_in[...]
    _, _, n_chip, _, half = wgrad_in.shape
    fhalf = wgrad_ref.shape[0] // 2
    for core in range(2):
        for chip in range(n_chip):
            count = min(r1, fhalf - chip * r1)
            if count > 0:
                start = core * fhalf + chip * r1
                for h in range(2):
                    wgrad_ref[start:start + count, h * half:(h + 1) * half] = (
                        wgrad_in[core, h, chip, 0:count, :].astype(F32) * scale
                    )


def per_device(features, node_order, weight, cotangent, tile_list, tile_values):
    n_blk, n_col = lax.axis_size("blk"), lax.axis_size("col")
    slots, tile, _ = tile_values.shape
    fin, hid = weight.shape
    n_chip = n_blk // 2
    half, fhalf = hid // 2, fin // 2
    scale = float(n_blk * n_col * tile) ** -0.5
    r1 = -(-fhalf // (16 * n_chip)) * 16
    r2 = -(-r1 // (16 * n_col)) * 16
    dma = lambda *n: pltpu.SemaphoreType.DMA(n)
    vmem = pltpu.VMEM
    wide, tall = n_blk * tile, n_col * tile
    turned = wide * tall <= 2 ** 21
    scratch = [
        vmem((tile, fin), BF16), vmem((1, tile), jnp.int32), vmem((fin, hid), BF16),
        vmem((tile, hid), BF16), vmem((slots, tile, tile), BF16),
        vmem((tile, hid), BF16), vmem((tile, fin), BF16),
        vmem((tall, wide), BF16), vmem((wide if turned else tile, tall), BF16),
        vmem((fin, tile), BF16), vmem((fhalf, wide), BF16),
        vmem((2, wide, half), BF16),
        vmem((2, tall, half), F32), vmem((2, tall, half), BF16), vmem((2, tall, half), BF16),
        vmem((2, tall, half), BF16),
        vmem((2, wide, half), F32), vmem((2, wide, half), BF16), vmem((2, wide, half), BF16),
        vmem((2, wide, half), BF16), vmem((2, n_chip * tile, half), BF16),
        vmem((2, n_chip * r1, half), F32), vmem((2, n_chip * r1, half), BF16),
        vmem((2, n_chip * r1, half), BF16),
        vmem((2, n_col * r2, half), F32), vmem((2, n_col * r2, half), BF16),
        vmem((2, n_col * r2, half), BF16), vmem((2, 2, n_chip, n_col * r2, half), BF16),
        dma(5), dma(3), dma(2, 2 * n_chip), dma(2, n_blk),
        dma(2, n_col), dma(2, n_col), dma(2, n_col), dma(2, n_col),
        dma(2), dma(2), dma(2, n_chip), dma(2, n_chip),
        dma(2 * n_chip), dma(n_blk), dma(2, n_chip), dma(2, n_chip),
        dma(2, n_col), dma(2, n_col), dma(2, n_col), dma(2, n_col),
        dma(2, n_chip), dma(2, n_chip), dma(2, n_chip), dma(2, n_chip),
    ]
    hbm = pl.BlockSpec(memory_space=pl.ANY)
    inside = pl.BlockSpec(memory_space=pltpu.VMEM)
    limit = 60 * 1024 * 1024
    hidden, xgrad, wgrad = pl.pallas_call(
        functools.partial(kernel, (n_blk, n_col, tile, fin, hid, r1, r2)),
        out_shape=(
            jax.ShapeDtypeStruct((tile, hid), BF16),
            jax.ShapeDtypeStruct((tile, fin), BF16),
            jax.ShapeDtypeStruct((2, 2, n_chip, r1, half), BF16),
        ),
        in_specs=[hbm, hbm, hbm, hbm, pl.BlockSpec(memory_space=pltpu.SMEM), hbm],
        out_specs=(hbm, hbm, hbm),
        scratch_shapes=scratch,
        compiler_params=pltpu.CompilerParams(
            collective_id=0, has_side_effects=True, vmem_limit_bytes=limit
        ),
        cost_estimate=pl.CostEstimate(
            flops=4 * slots * tile * tile * hid, bytes_accessed=4 * 1024 * 1024,
            transcendentals=tile * hid,
        ),
    )(features, node_order, weight, cotangent, tile_list.T, tile_values)
    return pl.pallas_call(
        functools.partial(finish, scale, r1),
        out_shape=(
            jax.ShapeDtypeStruct((tile, hid), BF16),
            jax.ShapeDtypeStruct((tile, fin), BF16),
            jax.ShapeDtypeStruct((fin, hid), F32),
        ),
        in_specs=[inside] * 3,
        out_specs=(inside,) * 3,
        compiler_params=pltpu.CompilerParams(vmem_limit_bytes=limit),
    )(hidden, xgrad, wgrad)


def solution(mesh):
    in_specs = (
        P(("blk", "col"), None),
        P(("blk", "col"), None),
        P(),
        P(("blk", "col"), None),
        P(("blk", "col"), None),
        P(("blk", "col"), None, None),
    )
    out_specs = (P(("blk", "col"), None), P(("blk", "col"), None), P())
    return jax.shard_map(
        per_device, mesh=mesh, in_specs=in_specs, out_specs=out_specs, check_vma=False
    )
```

time: 59.9 us -> 47.3 us (0.79)
  local copies, waits for them, and re-layouts: 6.51 us -> 0 us
  Pallas kernels: 52.4 us -> 46.5 us
    unnamed x4 -> x0, local copies, waits for them, and re-layouts: 6.51 us -> none
    pallas_call x1 -> x2, Pallas kernels: 52.4 us -> 46.5 us  [the longest x1 44.4 us: per_device(): pl.pallas_call(functools.partial(kernel, (n_blk, n_col, tile, fin, hid, r...]
where the time goes in v2:
time: 47.3 us; the launch traced here: 47.1 us
  Pallas kernels  46.5 us (98%)
  between operations  0.64 us (1%)
    pallas_call x1, Pallas kernels, per_device(): pl.pallas_call(functools.partial(kernel, (n_blk, n_col, tile, fin, hid, r...  44.4 us
    pallas_call x1, Pallas kernels, per_device(): pl.pallas_call(functools.partial(finish, scale, r1), out_shape=(jax.Shape...  2.11 us

profile of v2, /device:TPU:1, one launch (start us, length us, event | category | flops | bytes accessed | tf_op | source)
XLA Modules:
  0.0 47.1 jit_solution(4185910793167112674)
XLA Ops:
  0.6 44.4 %shard_map.85 = (bf16[128,256]{1,0:T(8,128)(2,1)}, bf16[128,768]{1,0:T(8,128)(2,1)}, bf16[2,2,4,96,128]{4,3,2,1,0:T(8,128)(2,1)}) custom-call(bf16[128,768]{1,0:T(8,128)(2,1)} %feat_h.1, s32[1,128]{1,0:T(1,128)} %order_h.1, bf16[768,256]{1,0:T(8,128)(2,1)} %weight_h.1, bf16[128,256]{1,0:T(8,128)(2,1)} %cot_h.1, s32[2,24]{1,0:T(2,128)} %bitcast.1, ...), custom_call_target="tpu_custom_call" | custom-call | flops 402653184 | bytes 4194304 | tf_op jit(solution)/shard_map/pallas_call | solution.py:340
  45.0 2.1 %shard_map.86 = (bf16[128,256]{1,0:T(8,128)(2,1)}, bf16[128,768]{1,0:T(8,128)(2,1)}, f32[768,256]{1,0:T(8,128)}) custom-call(bf16[128,256]{1,0:T(8,128)(2,1)} %get-tuple-element.6.hidden_in, bf16[128,768]{1,0:T(8,128)(2,1)} %get-tuple-element.7.xgrad_in, bf16[2,2,4,96,128]{4,3,2,1,0:T(8,128)(2,1)} %get-tuple-element.8.wgrad_in), custom_call_target="tpu_custom_call" | custom-call | tf_op jit(solution)/shard_map/pallas_call | solution.py:358

commit v3 on v2

--- a/solution.py
+++ b/solution.py
@@ -23,14 +23,15 @@
     hidden_h, xgrad_h, wgrad_h,
     feat, order, weight, cot, tiles, hidden, xgrad,
     adj, adj_t, feat_t, feat_all, panels, part, part16, agg_in, grads, pg_part, pg16,
-    pair_in, both16, chip_in, dw_sum, dw16, dw_chip, dw_mid, dw_mid16, dw_col, dw_all,
+    pair_in, both16, chip_in, dw_sum, dw16, dw_in, dw_mid, dw_mid16, dw_col, dw_all,
     in_sem, out_sem, ag_s, ag_r, rc_s, rc_r, gc_s, gc_r, pp_s, pp_r, pc_s, pc_r,
     fe_s, fe_r, dc_s, dc_r, dz_s, dz_r, dg_s, dg_r, dh_s, dh_r, di_s, di_r,
 ):
-    n_blk, n_col, tile, fin, hid, r1, r2 = dims
+    n_blk, n_col, tile, fin, hid, r1, r2, direct = dims
     n_chip = n_blk // 2
     half = hid // 2
     fhalf = fin // 2
+    n_own = fhalf // r1
     b = lax.axis_index("blk")
     c = lax.axis_index("col")
     chip = b // 2
@@ -41,13 +42,16 @@
     def rows(i, n=tile):
         return pl.ds(pl.multiple_of(i * n, n), n)
 
-    def send(src, dst, s_sem, r_sem, blk, col):
+    def send(src, dst, s_sem, r_sem, blk, col, only=None):
         copy = pltpu.make_async_remote_copy(
             src_ref=src, dst_ref=dst, send_sem=s_sem, recv_sem=r_sem,
             device_id=(blk, col), device_id_type=MESH,
         )
-        copy.start()
-        sends.append(copy)
+        if only is None:
+            copy.start()
+        else:
+            pl.when(only)(copy.start)
+        sends.append((copy, only))
 
     def arrive(dst, s_sem, r_sem):
         pltpu.make_async_remote_copy(
@@ -71,6 +75,8 @@
     peers += [(2 * to + core, c) for _, to, _ in chips]
     peers += [(2 * to + 1 - core, c) for _, to, _ in chips]
     peers += [(b, to) for _, to, _ in cols]
+    if direct:
+        peers += [(2 * to + core, at) for _, to, _ in chips for _, at, _ in cols]
     for peer in peers:
         pl.semaphore_signal(barrier, inc=1, device_id=peer, device_id_type=MESH)
 
@@ -172,7 +178,13 @@
     outs[0].start()
 
     bstep = 4 * tile if n_blk % 4 == 0 else tile
-    for h in range(2):
+    others = [
+        ((chip + i) % n_chip, (c + j) % n_col, (chip + n_chip - i) % n_chip, (c + n_col - j) % n_col)
+        for i in range(n_chip) for j in range(n_col) if i + j > 0
+    ]
+    mine = chip * n_col + c
+
+    def pair_start(h):
         for k, _, src in cols:
             arrive(grads.at[h, rows(src)], gc_s.at[h, k], gc_r.at[h, src])
 
@@ -191,38 +203,64 @@
         lax.fori_loop(0, n_blk * tile // bstep, backward, 0)
         send(pg16.at[h], pair_in.at[h], pp_s.at[h], pp_r.at[h], sib, c)
 
-    for k, _, src in chips:
-        for q in range(2):
-            at = feat_all.at[:, rows(2 * src + q)]
-            arrive(at, fe_s.at[0], fe_r.at[2 * src + q])
-    arrive(feat_all.at[:, rows(sib)], fe_s.at[0], fe_r.at[sib])
-
-    for h in range(2):
+    def features_arrive():
+        for k, _, src in chips:
+            for q in range(2):
+                at = feat_all.at[:, rows(2 * src + q)]
+                arrive(at, fe_s.at[0], fe_r.at[2 * src + q])
+        arrive(feat_all.at[:, rows(sib)], fe_s.at[0], fe_r.at[sib])
+
+    def terms_start(h):
         arrive(pair_in.at[h], pp_s.at[h], pp_r.at[h])
         both16[h] = (pg_part[h] + pair_in[h].astype(F32)).astype(BF16)
         term = dot(feat_all[...], both16[h])
         dw_sum[h, 0:fhalf, :] = term
         dw16[h, 0:fhalf, :] = term.astype(BF16)
+        if direct:
+            for i, (to, to_col, _, _) in enumerate(others):
+                owner = to * n_col + to_col
+                send(
+                    dw16.at[h, rows(owner, r1)], dw_in.at[h, rows(mine, r1)],
+                    dc_s.at[h, i], dc_r.at[h, mine], 2 * to + core, to_col, owner < n_own,
+                )
+            return
         if n_chip * r1 > fhalf:
             rest = jnp.zeros((n_chip * r1 - fhalf, half), F32)
             dw_sum[h, fhalf:, :] = rest
             dw16[h, fhalf:, :] = rest.astype(BF16)
         for k, to, _ in chips:
             send(
-                dw16.at[h, rows(to, r1)], dw_chip.at[h, rows(chip, r1)],
+                dw16.at[h, rows(to, r1)], dw_in.at[h, rows(chip, r1)],
                 dc_s.at[h, k], dc_r.at[h, chip], 2 * to + core, c,
             )
-    for h in range(2):
+
+    def owners_start(h):
         for k, to, _ in chips:
             send(
                 both16.at[h, rows(2 * to + core)], chip_in.at[h, rows(chip)],
                 pc_s.at[h, k], pc_r.at[h, chip], 2 * to + core, c,
             )
-    for h in range(2):
+
+    def result_start(h):
+        if direct:
+            @pl.when(mine < n_own)
+            def _():
+                piece = dw_sum[h, rows(mine, r1), :]
+                for i, (_, _, src, src_col) in enumerate(others):
+                    at = src * n_col + src_col
+                    arrive(dw_in.at[h, rows(at, r1)], dc_s.at[h, i], dc_r.at[h, at])
+                    piece = piece + dw_in[h, rows(at, r1), :].astype(F32)
+                dw_all[core, h, rows(mine, r1), :] = piece.astype(BF16)
+
+            at = dw_all.at[core, h, rows(mine, r1)]
+            for i, (to, to_col, _, _) in enumerate(others):
+                send(at, at, dg_s.at[h, i], dg_r.at[h, mine], 2 * to + core, to_col, mine < n_own)
+            send(at, at, di_s.at[h, mine], di_r.at[h, mine], sib, c, mine < n_own)
+            return
         piece = dw_sum[h, rows(chip, r1), :]
         for k, _, src in chips:
-            arrive(dw_chip.at[h, rows(src, r1)], dc_s.at[h, k], dc_r.at[h, src])
-            piece = piece + dw_chip[h, rows(src, r1), :].astype(F32)
+            arrive(dw_in.at[h, rows(src, r1)], dc_s.at[h, k], dc_r.at[h, src])
+            piece = piece + dw_in[h, rows(src, r1), :].astype(F32)
         dw_mid[h, 0:r1, :] = piece
         dw_mid16[h, 0:r1, :] = piece.astype(BF16)
         if n_col * r2 > r1:
@@ -234,7 +272,6 @@
                 dw_mid16.at[h, rows(to, r2)], dw_col.at[h, rows(c, r2)],
                 dz_s.at[h, k], dz_r.at[h, c], b, to,
             )
-    for h in range(2):
         piece = dw_mid[h, rows(c, r2), :]
         for k, _, src in cols:
             arrive(dw_col.at[h, rows(src, r2)], dz_s.at[h, k], dz_r.at[h, src])
@@ -243,42 +280,82 @@
         at = dw_all.at[core, h, chip, rows(c, r2)]
         for k, to, _ in cols:
             send(at, at, dg_s.at[h, k], dg_r.at[h, c], b, to)
-
-    sums = []
-    for h in range(2):
-        total = pg_part[h, rows(b), :] + pair_in[h, rows(b), :].astype(F32)
-        for k, _, src in chips:
-            arrive(chip_in.at[h, rows(src)], pc_s.at[h, k], pc_r.at[h, src])
-            total = total + chip_in[h, rows(src), :].astype(F32)
-        sums.append(total.astype(BF16))
-    back = dot(place, jnp.concatenate(sums, axis=1)).astype(BF16)
-    xgrad[...] = lax.dot_general(
-        back, weight[...], (((1,), (1,)), ((), ())), preferred_element_type=F32
-    ).astype(BF16)
-    outs.append(pltpu.make_async_copy(xgrad, xgrad_h, out_sem.at[1]))
-    outs[1].start()
-
-    for h in range(2):
         for k, _, src in cols:
             at = dw_all.at[core, h, chip, rows(src, r2)]
             arrive(at, dg_s.at[h, k], dg_r.at[h, src])
         at = dw_all.at[core, h, chip, pl.ds(0, r1)]
         for k, to, _ in chips:
             send(at, at, dh_s.at[h, k], dh_r.at[h, chip], 2 * to + core, c)
-        send(at, at, di_s.at[h, 0], di_r.at[h, chip], sib, c)
-    for h in range(2):
+        send(at, at, di_s.at[h, chip], di_r.at[h, chip], sib, c)
+
+    def result_pass(h):
+        if direct:
+            for i, (_, _, src, src_col) in enumerate(others):
+                owner = src * n_col + src_col
+                at = dw_all.at[core, h, rows(owner, r1)]
+
+                @pl.when(owner < n_own)
+                def _():
+                    arrive(at, dg_s.at[h, i], dg_r.at[h, owner])
+
+                send(at, at, di_s.at[h, owner], di_r.at[h, owner], sib, c, owner < n_own)
+            return
         for k, _, src in chips:
             at = dw_all.at[core, h, src, pl.ds(0, r1)]
             arrive(at, dh_s.at[h, k], dh_r.at[h, src])
-            send(at, at, di_s.at[h, k], di_r.at[h, src], sib, c)
-    for h in range(2):
-        for k, _, src in [(0, chip, chip)] + chips:
+            send(at, at, di_s.at[h, src], di_r.at[h, src], sib, c)
+
+    def result_arrive(h):
+        if direct:
+            for owner in range(n_own):
+                at = dw_all.at[1 - core, h, rows(owner, r1)]
+                arrive(at, di_s.at[h, owner], di_r.at[h, owner])
+            return
+        for src in range(n_chip):
             at = dw_all.at[1 - core, h, src, pl.ds(0, r1)]
-            arrive(at, di_s.at[h, k], di_r.at[h, src])
-    for copy in sends:
-        copy.wait_send()
-    outs.append(pltpu.make_async_copy(dw_all.at[:, :, :, pl.ds(0, r1)], wgrad_h, out_sem.at[2]))
+            arrive(at, di_s.at[h, src], di_r.at[h, src])
+
+    def own_features():
+        sums = []
+        for h in range(2):
+            total = pg_part[h, rows(b), :] + pair_in[h, rows(b), :].astype(F32)
+            for k, _, src in chips:
+                arrive(chip_in.at[h, rows(src)], pc_s.at[h, k], pc_r.at[h, src])
+                total = total + chip_in[h, rows(src), :].astype(F32)
+            sums.append(total.astype(BF16))
+        back = dot(place, jnp.concatenate(sums, axis=1)).astype(BF16)
+        xgrad[...] = lax.dot_general(
+            back, weight[...], (((1,), (1,)), ((), ())), preferred_element_type=F32
+        ).astype(BF16)
+        outs.append(pltpu.make_async_copy(xgrad, xgrad_h, out_sem.at[1]))
+        outs[1].start()
+
+    pair_start(0)
+    features_arrive()
+    terms_start(0)
+    owners_start(0)
+    pair_start(1)
+    result_start(0)
+    terms_start(1)
+    owners_start(1)
+    result_pass(0)
+    result_start(1)
+    own_features()
+    result_pass(1)
+    result_arrive(0)
+    result_arrive(1)
+    if direct:
+        outs.append(pltpu.make_async_copy(dw_all, wgrad_h, out_sem.at[2]))
+    else:
+        outs.append(
+            pltpu.make_async_copy(dw_all.at[:, :, :, pl.ds(0, r1)], wgrad_h, out_sem.at[2])
+        )
     outs[2].start()
+    for copy, only in sends:
+        if only is None:
+            copy.wait_send()
+        else:
+            pl.when(only)(copy.wait_send)
     for copy in outs:
         copy.wait()
 
@@ -286,16 +363,16 @@
 def finish(scale, r1, hidden_in, xgrad_in, wgrad_in, hidden_ref, xgrad_ref, wgrad_ref):
     hidden_ref[...] = hidden_in[...]
     xgrad_ref[...] = xgrad_in[...]
-    _, _, n_chip, _, half = wgrad_in.shape
+    n_part, half = wgrad_in.shape[2], wgrad_in.shape[4]
     fhalf = wgrad_ref.shape[0] // 2
     for core in range(2):
-        for chip in range(n_chip):
-            count = min(r1, fhalf - chip * r1)
+        for i in range(n_part):
+            count = min(r1, fhalf - i * r1)
             if count > 0:
-                start = core * fhalf + chip * r1
+                start = core * fhalf + i * r1
                 for h in range(2):
                     wgrad_ref[start:start + count, h * half:(h + 1) * half] = (
-                        wgrad_in[core, h, chip, 0:count, :].astype(F32) * scale
+                        wgrad_in[core, h, i, 0:count, :].astype(F32) * scale
                     )
 
 
@@ -306,8 +383,12 @@
     n_chip = n_blk // 2
     half, fhalf = hid // 2, fin // 2
     scale = float(n_blk * n_col * tile) ** -0.5
-    r1 = -(-fhalf // (16 * n_chip)) * 16
-    r2 = -(-r1 // (16 * n_col)) * 16
+    direct = n_chip * n_col <= 16
+    n_sum = n_chip * n_col if direct else n_chip
+    r1 = -(-fhalf // (16 * n_sum)) * 16
+    direct = direct and fhalf % r1 == 0
+    r2 = 16 if direct else -(-r1 // (16 * n_col)) * 16
+    padded = fhalf if direct else n_chip * r1
     dma = lambda *n: pltpu.SemaphoreType.DMA(n)
     vmem = pltpu.VMEM
     wide, tall = n_blk * tile, n_col * tile
@@ -323,29 +404,32 @@
         vmem((2, tall, half), BF16),
         vmem((2, wide, half), F32), vmem((2, wide, half), BF16), vmem((2, wide, half), BF16),
         vmem((2, wide, half), BF16), vmem((2, n_chip * tile, half), BF16),
-        vmem((2, n_chip * r1, half), F32), vmem((2, n_chip * r1, half), BF16),
-        vmem((2, n_chip * r1, half), BF16),
+        vmem((2, padded, half), F32), vmem((2, padded, half), BF16),
+        vmem((2, n_sum * r1, half), BF16),
         vmem((2, n_col * r2, half), F32), vmem((2, n_col * r2, half), BF16),
-        vmem((2, n_col * r2, half), BF16), vmem((2, 2, n_chip, n_col * r2, half), BF16),
+        vmem((2, n_col * r2, half), BF16), vmem((2, 2, fhalf, half) if direct else (2, 2, n_chip, n_col * r2, half), BF16),
         dma(5), dma(3), dma(2, 2 * n_chip), dma(2, n_blk),
         dma(2, n_col), dma(2, n_col), dma(2, n_col), dma(2, n_col),
         dma(2), dma(2), dma(2, n_chip), dma(2, n_chip),
-        dma(2 * n_chip), dma(n_blk), dma(2, n_chip), dma(2, n_chip),
-        dma(2, n_col), dma(2, n_col), dma(2, n_col), dma(2, n_col),
-        dma(2, n_chip), dma(2, n_chip), dma(2, n_chip), dma(2, n_chip),
+        dma(2 * n_chip), dma(n_blk), dma(2, n_sum), dma(2, n_sum),
+        dma(2, n_col), dma(2, n_col), dma(2, n_sum + n_col), dma(2, n_sum + n_col),
+        dma(2, n_chip), dma(2, n_chip), dma(2, n_sum), dma(2, n_sum),
     ]
-    hbm = pl.BlockSpec(memory_space=pl.ANY)
+    far = pl.BlockSpec(memory_space=pltpu.HBM)
+    free = pl.BlockSpec(memory_space=pl.ANY)
     inside = pl.BlockSpec(memory_space=pltpu.VMEM)
     limit = 60 * 1024 * 1024
     hidden, xgrad, wgrad = pl.pallas_call(
-        functools.partial(kernel, (n_blk, n_col, tile, fin, hid, r1, r2)),
+        functools.partial(kernel, (n_blk, n_col, tile, fin, hid, r1, r2, direct)),
         out_shape=(
             jax.ShapeDtypeStruct((tile, hid), BF16),
             jax.ShapeDtypeStruct((tile, fin), BF16),
-            jax.ShapeDtypeStruct((2, 2, n_chip, r1, half), BF16),
+            jax.ShapeDtypeStruct(
+                (2, 2, fhalf, half) if direct else (2, 2, n_chip, r1, half), BF16
+            ),
         ),
-        in_specs=[hbm, hbm, hbm, hbm, pl.BlockSpec(memory_space=pltpu.SMEM), hbm],
-        out_specs=(hbm, hbm, hbm),
+        in_specs=[far, far, far, far, pl.BlockSpec(memory_space=pltpu.SMEM), far],
+        out_specs=(free, free, free),
         scratch_shapes=scratch,
         compiler_params=pltpu.CompilerParams(
             collective_id=0, has_side_effects=True, vmem_limit_bytes=limit
@@ -355,6 +439,8 @@
             transcendentals=tile * hid,
         ),
     )(features, node_order, weight, cotangent, tile_list.T, tile_values)
+    if direct:
+        wgrad, r1 = wgrad.reshape(2, 2, 1, fhalf, half), fhalf
     return pl.pallas_call(
         functools.partial(finish, scale, r1),
         out_shape=(

time: 47.3 us -> 51 us (1.078)
  Pallas kernels: 46.5 us -> 50.2 us
    pallas_call x1, Pallas kernels: 44.4 us -> 48.1 us  [per_device(): pl.pallas_call(functools.partial(kernel, (n_blk, n_col, tile, fin, hid, r...]
where the time goes in v3:
time: 51 us; the launch traced here: 50.8 us
  Pallas kernels  50.2 us (98%)
  between operations  0.64 us (1%)
    pallas_call x1, Pallas kernels, per_device(): pl.pallas_call(functools.partial(kernel, (n_blk, n_col, tile, fin, hid, r...  48.1 us
    pallas_call x1, Pallas kernels, per_device(): pl.pallas_call(functools.partial(finish, scale, r1), out_shape=(jax.Shape...  2.11 us

profile of v3, /device:TPU:1, one launch (start us, length us, event | category | flops | bytes accessed | tf_op | source)
XLA Modules:
  0.0 50.8 jit_solution(9093435196807631864)
XLA Ops:
  0.6 48.1 %shard_map.85 = (bf16[128,256]{1,0:T(8,128)(2,1)}, bf16[128,768]{1,0:T(8,128)(2,1)}, bf16[2,2,384,128]{3,2,1,0:T(8,128)(2,1)}) custom-call(bf16[128,768]{1,0:T(8,128)(2,1)} %feat_h.1, s32[1,128]{1,0:T(1,128)} %order_h.1, bf16[768,256]{1,0:T(8,128)(2,1)} %weight_h.1, bf16[128,256]{1,0:T(8,128)(2,1)} %cot_h.1, s32[2,24]{1,0:T(2,128)} %bitcast.3, ...), custom_call_target="tpu_custom_call" | custom-call | flops 402653184 | bytes 4194304 | tf_op jit(solution)/shard_map/pallas_call | solution.py:422
  48.7 2.1 %shard_map.86 = (bf16[128,256]{1,0:T(8,128)(2,1)}, bf16[128,768]{1,0:T(8,128)(2,1)}, f32[768,256]{1,0:T(8,128)}) custom-call(bf16[128,256]{1,0:T(8,128)(2,1)} %get-tuple-element.6.hidden_in, bf16[128,768]{1,0:T(8,128)(2,1)} %get-tuple-element.7.xgrad_in, bf16[2,2,1,384,128]{4,3,2,1,0:T(8,128)(2,1)} %bitcast.2), custom_call_target="tpu_custom_call" | custom-call | tf_op jit(solution)/shard_map/pallas_call | solution.py:444

commit v4 on v3

--- a/solution.py
+++ b/solution.py
@@ -383,7 +383,7 @@
     n_chip = n_blk // 2
     half, fhalf = hid // 2, fin // 2
     scale = float(n_blk * n_col * tile) ** -0.5
-    direct = n_chip * n_col <= 16
+    direct = False
     n_sum = n_chip * n_col if direct else n_chip
     r1 = -(-fhalf // (16 * n_sum)) * 16
     direct = direct and fhalf % r1 == 0

time: 51 us -> 56.1 us (1.10)
  Pallas kernels: 50.2 us -> 55.2 us
    pallas_call x1, Pallas kernels: 48.1 us -> 53.1 us  [per_device(): pl.pallas_call(functools.partial(kernel, (n_blk, n_col, tile, fin, hid, r...]
where the time goes in v4:
time: 56.1 us; the launch traced here: 55.9 us
  Pallas kernels  55.2 us (98%)
  between operations  0.64 us (1%)
    pallas_call x1, Pallas kernels, per_device(): pl.pallas_call(functools.partial(kernel, (n_blk, n_col, tile, fin, hid, r...  53.1 us
    pallas_call x1, Pallas kernels, per_device(): pl.pallas_call(functools.partial(finish, scale, r1), out_shape=(jax.Shape...  2.11 us

profile of v4, /device:TPU:1, one launch (start us, length us, event | category | flops | bytes accessed | tf_op | source)
XLA Modules:
  0.0 55.9 jit_solution(1272973917355959123)
XLA Ops:
  0.6 53.1 %shard_map.85 = (bf16[128,256]{1,0:T(8,128)(2,1)}, bf16[128,768]{1,0:T(8,128)(2,1)}, bf16[2,2,4,96,128]{4,3,2,1,0:T(8,128)(2,1)}) custom-call(bf16[128,768]{1,0:T(8,128)(2,1)} %feat_h.1, s32[1,128]{1,0:T(1,128)} %order_h.1, bf16[768,256]{1,0:T(8,128)(2,1)} %weight_h.1, bf16[128,256]{1,0:T(8,128)(2,1)} %cot_h.1, s32[2,24]{1,0:T(2,128)} %bitcast.1, ...), custom_call_target="tpu_custom_call" | custom-call | flops 402653184 | bytes 4194304 | tf_op jit(solution)/shard_map/pallas_call | solution.py:422
  53.8 2.1 %shard_map.86 = (bf16[128,256]{1,0:T(8,128)(2,1)}, bf16[128,768]{1,0:T(8,128)(2,1)}, f32[768,256]{1,0:T(8,128)}) custom-call(bf16[128,256]{1,0:T(8,128)(2,1)} %get-tuple-element.6.hidden_in, bf16[128,768]{1,0:T(8,128)(2,1)} %get-tuple-element.7.xgrad_in, bf16[2,2,4,96,128]{4,3,2,1,0:T(8,128)(2,1)} %get-tuple-element.8.wgrad_in), custom_call_target="tpu_custom_call" | custom-call | tf_op jit(solution)/shard_map/pallas_call | solution.py:444

commit v5 on v3

--- a/solution.py
+++ b/solution.py
@@ -331,16 +331,16 @@
         outs[1].start()
 
     pair_start(0)
+    pair_start(1)
     features_arrive()
     terms_start(0)
+    terms_start(1)
     owners_start(0)
-    pair_start(1)
+    owners_start(1)
     result_start(0)
-    terms_start(1)
-    owners_start(1)
-    result_pass(0)
     result_start(1)
     own_features()
+    result_pass(0)
     result_pass(1)
     result_arrive(0)
     result_arrive(1)

time: 51 us -> 47.2 us (0.925)
  Pallas kernels: 50.2 us -> 46.4 us
    pallas_call x1, Pallas kernels: 48.1 us -> 44.3 us  [per_device(): pl.pallas_call(functools.partial(kernel, (n_blk, n_col, tile, fin, hid, r...]
where the time goes in v5:
time: 47.2 us; the launch traced here: 47 us
  Pallas kernels  46.4 us (98%)
  between operations  0.64 us (1%)
    pallas_call x1, Pallas kernels, per_device(): pl.pallas_call(functools.partial(kernel, (n_blk, n_col, tile, fin, hid, r...  44.3 us
    pallas_call x1, Pallas kernels, per_device(): pl.pallas_call(functools.partial(finish, scale, r1), out_shape=(jax.Shape...  2.11 us

profile of v5, /device:TPU:1, one launch (start us, length us, event | category | flops | bytes accessed | tf_op | source)
XLA Modules:
  0.0 47.0 jit_solution(8531899961990932586)
XLA Ops:
  0.6 44.3 %shard_map.85 = (bf16[128,256]{1,0:T(8,128)(2,1)}, bf16[128,768]{1,0:T(8,128)(2,1)}, bf16[2,2,384,128]{3,2,1,0:T(8,128)(2,1)}) custom-call(bf16[128,768]{1,0:T(8,128)(2,1)} %feat_h.1, s32[1,128]{1,0:T(1,128)} %order_h.1, bf16[768,256]{1,0:T(8,128)(2,1)} %weight_h.1, bf16[128,256]{1,0:T(8,128)(2,1)} %cot_h.1, s32[2,24]{1,0:T(2,128)} %bitcast.3, ...), custom_call_target="tpu_custom_call" | custom-call | flops 402653184 | bytes 4194304 | tf_op jit(solution)/shard_map/pallas_call | solution.py:422
  44.9 2.1 %shard_map.86 = (bf16[128,256]{1,0:T(8,128)(2,1)}, bf16[128,768]{1,0:T(8,128)(2,1)}, f32[768,256]{1,0:T(8,128)}) custom-call(bf16[128,256]{1,0:T(8,128)(2,1)} %get-tuple-element.6.hidden_in, bf16[128,768]{1,0:T(8,128)(2,1)} %get-tuple-element.7.xgrad_in, bf16[2,2,1,384,128]{4,3,2,1,0:T(8,128)(2,1)} %bitcast.2), custom_call_target="tpu_custom_call" | custom-call | tf_op jit(solution)/shard_map/pallas_call | solution.py:444

commit v6 on v5

--- a/solution.py
+++ b/solution.py
@@ -100,6 +100,17 @@
             send(at, at, ag_s.at[h, k], ag_r.at[h, b], 2 * to + core, c)
         send(at, at, ag_s.at[h, 0], ag_r.at[h, b], sib, c)
 
+    feat_t[...] = lax.dot_general(
+        feat[...], place, (((0,), (0,)), ((), ())), preferred_element_type=F32
+    ).astype(BF16)
+    feat_all[:, rows(b)] = feat_t[rows(core, fhalf), :]
+
+    for k, to, _ in chips:
+        for q in range(2):
+            at = feat_all.at[:, rows(b)]
+            send(feat_t.at[pl.ds(q * fhalf, fhalf)], at, fe_s.at[2 * k + q], fe_r.at[b], 2 * to + q, c)
+    send(feat_t.at[rows(1 - core, fhalf)], feat_all.at[:, rows(b)], fe_s.at[0], fe_r.at[b], sib, c)
+
     loads[3].wait()
 
     def build(g, _):
@@ -113,11 +124,6 @@
         return 0
 
     lax.fori_loop(0, n_blk, build, 0)
-    feat_t[...] = lax.dot_general(
-        feat[...], place, (((0,), (0,)), ((), ())), preferred_element_type=F32
-    ).astype(BF16)
-    feat_all[:, rows(b)] = feat_t[rows(core, fhalf), :]
-
     step = 4 * tile if n_col % 4 == 0 else tile
     for h in range(2):
         for k, _, src in chips:
@@ -138,12 +144,6 @@
         lax.fori_loop(0, n_col * tile // step, forward, 0)
         for k, to, _ in cols:
             send(part16.at[h, rows(to)], agg_in.at[h, rows(c)], rc_s.at[h, k], rc_r.at[h, c], b, to)
-
-    for k, to, _ in chips:
-        for q in range(2):
-            at = feat_all.at[:, rows(b)]
-            send(feat_t.at[pl.ds(q * fhalf, fhalf)], at, fe_s.at[2 * k + q], fe_r.at[b], 2 * to + q, c)
-    send(feat_t.at[rows(1 - core, fhalf)], feat_all.at[:, rows(b)], fe_s.at[0], fe_r.at[b], sib, c)
 
     def turn(g, _):
         for r in range(n_col):

time: 47.2 us -> 48.9 us (1.036)
  Pallas kernels: 46.4 us -> 48.1 us
    pallas_call x1, Pallas kernels: 44.3 us -> 46 us  [per_device(): pl.pallas_call(functools.partial(kernel, (n_blk, n_col, tile, fin, hid, r...]
where the time goes in v6:
time: 48.9 us; the launch traced here: 48.7 us
  Pallas kernels  48.1 us (98%)
  between operations  0.64 us (1%)
    pallas_call x1, Pallas kernels, per_device(): pl.pallas_call(functools.partial(kernel, (n_blk, n_col, tile, fin, hid, r...  46 us
    pallas_call x1, Pallas kernels, per_device(): pl.pallas_call(functools.partial(finish, scale, r1), out_shape=(jax.Shape...  2.11 us

profile of v6, /device:TPU:1, one launch (start us, length us, event | category | flops | bytes accessed | tf_op | source)
XLA Modules:
  0.0 48.7 jit_solution(17413214884700884911)
XLA Ops:
  0.6 46.0 %shard_map.85 = (bf16[128,256]{1,0:T(8,128)(2,1)}, bf16[128,768]{1,0:T(8,128)(2,1)}, bf16[2,2,384,128]{3,2,1,0:T(8,128)(2,1)}) custom-call(bf16[128,768]{1,0:T(8,128)(2,1)} %feat_h.1, s32[1,128]{1,0:T(1,128)} %order_h.1, bf16[768,256]{1,0:T(8,128)(2,1)} %weight_h.1, bf16[128,256]{1,0:T(8,128)(2,1)} %cot_h.1, s32[2,24]{1,0:T(2,128)} %bitcast.3, ...), custom_call_target="tpu_custom_call" | custom-call | flops 402653184 | bytes 4194304 | tf_op jit(solution)/shard_map/pallas_call | solution.py:422
  46.6 2.1 %shard_map.86 = (bf16[128,256]{1,0:T(8,128)(2,1)}, bf16[128,768]{1,0:T(8,128)(2,1)}, f32[768,256]{1,0:T(8,128)}) custom-call(bf16[128,256]{1,0:T(8,128)(2,1)} %get-tuple-element.6.hidden_in, bf16[128,768]{1,0:T(8,128)(2,1)} %get-tuple-element.7.xgrad_in, bf16[2,2,1,384,128]{4,3,2,1,0:T(8,128)(2,1)} %bitcast.2), custom_call_target="tpu_custom_call" | custom-call | tf_op jit(solution)/shard_map/pallas_call | solution.py:444

commit v7 on v6

--- a/solution.py
+++ b/solution.py
@@ -42,7 +42,7 @@
     def rows(i, n=tile):
         return pl.ds(pl.multiple_of(i * n, n), n)
 
-    def send(src, dst, s_sem, r_sem, blk, col, only=None):
+    def send(src, dst, s_sem, r_sem, blk, col, only=None, keep=True):
         copy = pltpu.make_async_remote_copy(
             src_ref=src, dst_ref=dst, send_sem=s_sem, recv_sem=r_sem,
             device_id=(blk, col), device_id_type=MESH,
@@ -51,13 +51,20 @@
             copy.start()
         else:
             pl.when(only)(copy.start)
-        sends.append((copy, only))
+        if keep:
+            sends.append((copy, only))
 
     def arrive(dst, s_sem, r_sem):
         pltpu.make_async_remote_copy(
             src_ref=dst, dst_ref=dst, send_sem=s_sem, recv_sem=r_sem,
             device_id=(sib, c), device_id_type=MESH,
         ).wait_recv()
+
+    def sent(like, s_sem):
+        pltpu.make_async_remote_copy(
+            src_ref=like, dst_ref=like, send_sem=s_sem, recv_sem=pp_r.at[0],
+            device_id=(sib, c), device_id_type=MESH,
+        ).wait_send()
 
     chips = [(k, (chip + k) % n_chip, (chip + n_chip - k) % n_chip) for k in range(1, n_chip)]
     cols = [(k, (c + k) % n_col, (c + n_col - k) % n_col) for k in range(1, n_col)]
@@ -97,19 +104,13 @@
     for h in range(2):
         at = panels.at[h, rows(b)]
         for k, to, _ in chips:
-            send(at, at, ag_s.at[h, k], ag_r.at[h, b], 2 * to + core, c)
-        send(at, at, ag_s.at[h, 0], ag_r.at[h, b], sib, c)
+            send(at, at, ag_s.at[h, 0], ag_r.at[h, b], 2 * to + core, c, keep=False)
+        send(at, at, ag_s.at[h, 0], ag_r.at[h, sib], sib, c, keep=False)
 
     feat_t[...] = lax.dot_general(
         feat[...], place, (((0,), (0,)), ((), ())), preferred_element_type=F32
     ).astype(BF16)
     feat_all[:, rows(b)] = feat_t[rows(core, fhalf), :]
-
-    for k, to, _ in chips:
-        for q in range(2):
-            at = feat_all.at[:, rows(b)]
-            send(feat_t.at[pl.ds(q * fhalf, fhalf)], at, fe_s.at[2 * k + q], fe_r.at[b], 2 * to + q, c)
-    send(feat_t.at[rows(1 - core, fhalf)], feat_all.at[:, rows(b)], fe_s.at[0], fe_r.at[b], sib, c)
 
     loads[3].wait()
 
@@ -128,12 +129,9 @@
     for h in range(2):
         for k, _, src in chips:
             at = panels.at[h, rows(2 * src + core)]
-            arrive(at, ag_s.at[h, k], ag_r.at[h, 2 * src + core])
-            send(at, at, ag_s.at[h, n_chip + k], ag_r.at[h, 2 * src + core], sib, c)
-        arrive(panels.at[h, rows(sib)], ag_s.at[h, 0], ag_r.at[h, sib])
-        for k, _, src in chips:
-            at = 2 * src + 1 - core
-            arrive(panels.at[h, rows(at)], ag_s.at[h, k], ag_r.at[h, at])
+            arrive(at, ag_s.at[h, 0], ag_r.at[h, 2 * src + core])
+            send(at, at, ag_s.at[h, 0], ag_r.at[h, sib], sib, c, keep=False)
+        arrive(panels.at[h, pl.ds(0, n_chip * tile)], ag_s.at[h, 0], ag_r.at[h, b])
 
         def forward(i, _):
             got = dot(adj[rows(i, step), :], panels[h])
@@ -143,7 +141,19 @@
 
         lax.fori_loop(0, n_col * tile // step, forward, 0)
         for k, to, _ in cols:
-            send(part16.at[h, rows(to)], agg_in.at[h, rows(c)], rc_s.at[h, k], rc_r.at[h, c], b, to)
+            send(
+                part16.at[h, rows(to)], agg_in.at[h, rows(c)], rc_s.at[h, 0], rc_r.at[h, 0], b, to,
+                keep=False,
+            )
+
+    for k, to, _ in chips:
+        for q in range(2):
+            at = feat_all.at[:, rows(b)]
+            send(feat_t.at[pl.ds(q * fhalf, fhalf)], at, fe_s.at[0], fe_r.at[0], 2 * to + q, c, keep=False)
+    send(
+        feat_t.at[rows(1 - core, fhalf)], feat_all.at[:, rows(b)], fe_s.at[0], fe_r.at[0], sib, c,
+        keep=False,
+    )
 
     def turn(g, _):
         for r in range(n_col):
@@ -160,8 +170,8 @@
     root = 0.7978845608028654
     for h in range(2):
         agg = part[h, rows(c), :]
+        arrive(agg_in.at[h, pl.ds(0, (n_col - 1) * tile)], rc_s.at[h, 0], rc_r.at[h, 0])
         for k, _, src in cols:
-            arrive(agg_in.at[h, rows(src)], rc_s.at[h, k], rc_r.at[h, src])
             agg = agg + agg_in[h, rows(src), :].astype(F32)
         inner = root * (agg + 0.044715 * agg * agg * agg)
         th = jnp.tanh(inner)
@@ -172,10 +182,13 @@
         grads[h, rows(c), :] = (cot[:, lanes].astype(F32) * slope).astype(BF16)
         at = grads.at[h, rows(c)]
         for k, to, _ in cols:
-            send(at, at, gc_s.at[h, k], gc_r.at[h, c], b, to)
+            send(at, at, gc_s.at[h, 0], gc_r.at[h, 0], b, to, keep=False)
         hidden[:, lanes] = (0.5 * agg * (1.0 + th)).astype(BF16)
     outs = [pltpu.make_async_copy(hidden, hidden_h, out_sem.at[0])]
     outs[0].start()
+    for h in range(2):
+        sent(panels.at[h, pl.ds(0, (n_blk - 1) * tile)], ag_s.at[h, 0])
+        sent(part16.at[h, pl.ds(0, (n_col - 1) * tile)], rc_s.at[h, 0])
 
     bstep = 4 * tile if n_blk % 4 == 0 else tile
     others = [
@@ -185,8 +198,7 @@
     mine = chip * n_col + c
 
     def pair_start(h):
-        for k, _, src in cols:
-            arrive(grads.at[h, rows(src)], gc_s.at[h, k], gc_r.at[h, src])
+        arrive(grads.at[h, pl.ds(0, (n_col - 1) * tile)], gc_s.at[h, 0], gc_r.at[h, 0])
 
         def backward(i, _):
             if turned:
@@ -204,59 +216,72 @@
         send(pg16.at[h], pair_in.at[h], pp_s.at[h], pp_r.at[h], sib, c)
 
     def features_arrive():
-        for k, _, src in chips:
-            for q in range(2):
-                at = feat_all.at[:, rows(2 * src + q)]
-                arrive(at, fe_s.at[0], fe_r.at[2 * src + q])
-        arrive(feat_all.at[:, rows(sib)], fe_s.at[0], fe_r.at[sib])
-
-    def terms_start(h):
-        arrive(pair_in.at[h], pp_s.at[h], pp_r.at[h])
-        both16[h] = (pg_part[h] + pair_in[h].astype(F32)).astype(BF16)
-        term = dot(feat_all[...], both16[h])
-        dw_sum[h, 0:fhalf, :] = term
-        dw16[h, 0:fhalf, :] = term.astype(BF16)
+        arrive(feat_all.at[:, pl.ds(0, (n_blk - 1) * tile)], fe_s.at[0], fe_r.at[0])
+
+    def terms_start():
+        for h in range(2):
+            arrive(pair_in.at[h], pp_s.at[h], pp_r.at[h])
+            both16[h] = (pg_part[h] + pair_in[h].astype(F32)).astype(BF16)
+        for h in range(2):
+            term = dot(feat_all[...], both16[h])
+            dw_sum[h, 0:fhalf, :] = term
+            dw16[h, 0:fhalf, :] = term.astype(BF16)
+            if n_chip * r1 > fhalf and not direct:
+                rest = jnp.zeros((n_chip * r1 - fhalf, half), F32)
+                dw_sum[h, fhalf:, :] = rest
+                dw16[h, fhalf:, :] = rest.astype(BF16)
         if direct:
-            for i, (to, to_col, _, _) in enumerate(others):
+            for to, to_col, _, _ in others:
                 owner = to * n_col + to_col
                 send(
-                    dw16.at[h, rows(owner, r1)], dw_in.at[h, rows(mine, r1)],
-                    dc_s.at[h, i], dc_r.at[h, mine], 2 * to + core, to_col, owner < n_own,
+                    dw16.at[:, rows(owner, r1)], dw_in.at[:, rows(mine, r1)],
+                    dc_s.at[0, 0], dc_r.at[0, 0], 2 * to + core, to_col, owner < n_own, keep=False,
                 )
             return
-        if n_chip * r1 > fhalf:
-            rest = jnp.zeros((n_chip * r1 - fhalf, half), F32)
-            dw_sum[h, fhalf:, :] = rest
-            dw16[h, fhalf:, :] = rest.astype(BF16)
+        for h in range(2):
+            for k, to, _ in chips:
+                send(
+                    dw16.at[h, rows(to, r1)], dw_in.at[h, rows(chip, r1)],
+                    dc_s.at[h, k], dc_r.at[h, chip], 2 * to + core, c,
+                )
+
+    def owners_start():
         for k, to, _ in chips:
             send(
-                dw16.at[h, rows(to, r1)], dw_in.at[h, rows(chip, r1)],
-                dc_s.at[h, k], dc_r.at[h, chip], 2 * to + core, c,
+                both16.at[:, rows(2 * to + core)], chip_in.at[:, rows(chip)],
+                pc_s.at[0, 0], pc_r.at[0, 0], 2 * to + core, c, keep=False,
             )
 
-    def owners_start(h):
-        for k, to, _ in chips:
+    def result_direct():
+        count = len(others) * r1
+
+        @pl.when(mine < n_own)
+        def _():
+            arrive(dw_in.at[:, pl.ds(0, count)], dc_s.at[0, 0], dc_r.at[0, 0])
+            piece = dw_sum[:, rows(mine, r1), :]
+            for _, _, src, src_col in others:
+                piece = piece + dw_in[:, rows(src * n_col + src_col, r1), :].astype(F32)
+            dw_all[core, :, rows(mine, r1), :] = piece.astype(BF16)
+
+        at = dw_all.at[core, :, rows(mine, r1)]
+        for to, to_col, _, _ in others:
             send(
-                both16.at[h, rows(2 * to + core)], chip_in.at[h, rows(chip)],
-                pc_s.at[h, k], pc_r.at[h, chip], 2 * to + core, c,
+                at, at, dg_s.at[0, 0], dg_r.at[0, 0], 2 * to + core, to_col, mine < n_own,
+                keep=False,
             )
 
+    def pass_direct():
+        for owns in range(2):
+            rest = (n_own - owns) * r1
+
+            @pl.when((mine < n_own) == bool(owns))
+            def _():
+                sent(dw16.at[:, pl.ds(0, rest)], dc_s.at[0, 0])
+                arrive(dw_all.at[core, :, pl.ds(0, rest)], dg_s.at[0, 0], dg_r.at[0, 0])
+
+        send(dw_all.at[core], dw_all.at[core], di_s.at[0, 0], di_r.at[0, 0], sib, c)
+
     def result_start(h):
-        if direct:
-            @pl.when(mine < n_own)
-            def _():
-                piece = dw_sum[h, rows(mine, r1), :]
-                for i, (_, _, src, src_col) in enumerate(others):
-                    at = src * n_col + src_col
-                    arrive(dw_in.at[h, rows(at, r1)], dc_s.at[h, i], dc_r.at[h, at])
-                    piece = piece + dw_in[h, rows(at, r1), :].astype(F32)
-                dw_all[core, h, rows(mine, r1), :] = piece.astype(BF16)
-
-            at = dw_all.at[core, h, rows(mine, r1)]
-            for i, (to, to_col, _, _) in enumerate(others):
-                send(at, at, dg_s.at[h, i], dg_r.at[h, mine], 2 * to + core, to_col, mine < n_own)
-            send(at, at, di_s.at[h, mine], di_r.at[h, mine], sib, c, mine < n_own)
-            return
         piece = dw_sum[h, rows(chip, r1), :]
         for k, _, src in chips:
             arrive(dw_in.at[h, rows(src, r1)], dc_s.at[h, k], dc_r.at[h, src])
@@ -289,38 +314,22 @@
         send(at, at, di_s.at[h, chip], di_r.at[h, chip], sib, c)
 
     def result_pass(h):
-        if direct:
-            for i, (_, _, src, src_col) in enumerate(others):
-                owner = src * n_col + src_col
-                at = dw_all.at[core, h, rows(owner, r1)]
-
-                @pl.when(owner < n_own)
-                def _():
-                    arrive(at, dg_s.at[h, i], dg_r.at[h, owner])
-
-                send(at, at, di_s.at[h, owner], di_r.at[h, owner], sib, c, owner < n_own)
-            return
         for k, _, src in chips:
             at = dw_all.at[core, h, src, pl.ds(0, r1)]
             arrive(at, dh_s.at[h, k], dh_r.at[h, src])
             send(at, at, di_s.at[h, src], di_r.at[h, src], sib, c)
 
     def result_arrive(h):
-        if direct:
-            for owner in range(n_own):
-                at = dw_all.at[1 - core, h, rows(owner, r1)]
-                arrive(at, di_s.at[h, owner], di_r.at[h, owner])
-            return
         for src in range(n_chip):
             at = dw_all.at[1 - core, h, src, pl.ds(0, r1)]
             arrive(at, di_s.at[h, src], di_r.at[h, src])
 
     def own_features():
         sums = []
+        arrive(chip_in.at[:, pl.ds(0, (n_chip - 1) * tile)], pc_s.at[0, 0], pc_r.at[0, 0])
         for h in range(2):
             total = pg_part[h, rows(b), :] + pair_in[h, rows(b), :].astype(F32)
             for k, _, src in chips:
-                arrive(chip_in.at[h, rows(src)], pc_s.at[h, k], pc_r.at[h, src])
                 total = total + chip_in[h, rows(src), :].astype(F32)
             sums.append(total.astype(BF16))
         back = dot(place, jnp.concatenate(sums, axis=1)).astype(BF16)
@@ -333,17 +342,24 @@
     pair_start(0)
     pair_start(1)
     features_arrive()
-    terms_start(0)
-    terms_start(1)
-    owners_start(0)
-    owners_start(1)
-    result_start(0)
-    result_start(1)
-    own_features()
-    result_pass(0)
-    result_pass(1)
-    result_arrive(0)
-    result_arrive(1)
+    terms_start()
+    owners_start()
+    for h in range(2):
+        sent(grads.at[h, pl.ds(0, (n_col - 1) * tile)], gc_s.at[h, 0])
+    sent(feat_all.at[:, pl.ds(0, (n_blk - 1) * tile)], fe_s.at[0])
+    if direct:
+        result_direct()
+        own_features()
+        pass_direct()
+        arrive(dw_all.at[1 - core], di_s.at[0, 0], di_r.at[0, 0])
+    else:
+        result_start(0)
+        result_start(1)
+        own_features()
+        result_pass(0)
+        result_pass(1)
+        result_arrive(0)
+        result_arrive(1)
     if direct:
         outs.append(pltpu.make_async_copy(dw_all, wgrad_h, out_sem.at[2]))
     else:
@@ -351,6 +367,12 @@
             pltpu.make_async_copy(dw_all.at[:, :, :, pl.ds(0, r1)], wgrad_h, out_sem.at[2])
         )
     outs[2].start()
+    sent(both16.at[:, pl.ds(0, (n_chip - 1) * tile)], pc_s.at[0, 0])
+    if direct:
+        @pl.when(mine < n_own)
+        def _():
+            sent(dw_in.at[:, pl.ds(0, len(others) * r1)], dg_s.at[0, 0])
+
     for copy, only in sends:
         if only is None:
             copy.wait_send()

time: 48.9 us -> 50.6 us (1.035)
  Pallas kernels: 48.1 us -> 49.7 us
    pallas_call x1, Pallas kernels: 46 us -> 47.6 us  [per_device(): pl.pallas_call(functools.partial(kernel, (n_blk, n_col, tile, fin, hid, r...]
where the time goes in v7:
time: 50.6 us; the launch traced here: 50.4 us
  Pallas kernels  49.7 us (98%)
  between operations  0.64 us (1%)
    pallas_call x1, Pallas kernels, per_device(): pl.pallas_call(functools.partial(kernel, (n_blk, n_col, tile, fin, hid, r...  47.6 us
    pallas_call x1, Pallas kernels, per_device(): pl.pallas_call(functools.partial(finish, scale, r1), out_shape=(jax.Shape...  2.11 us

profile of v7, /device:TPU:1, one launch (start us, length us, event | category | flops | bytes accessed | tf_op | source)
XLA Modules:
  0.0 50.4 jit_solution(4170493987658368135)
XLA Ops:
  0.6 47.6 %shard_map.85 = (bf16[128,256]{1,0:T(8,128)(2,1)}, bf16[128,768]{1,0:T(8,128)(2,1)}, bf16[2,2,384,128]{3,2,1,0:T(8,128)(2,1)}) custom-call(bf16[128,768]{1,0:T(8,128)(2,1)} %feat_h.1, s32[1,128]{1,0:T(1,128)} %order_h.1, bf16[768,256]{1,0:T(8,128)(2,1)} %weight_h.1, bf16[128,256]{1,0:T(8,128)(2,1)} %cot_h.1, s32[2,24]{1,0:T(2,128)} %bitcast.3, ...), custom_call_target="tpu_custom_call" | custom-call | flops 402653184 | bytes 4194304 | tf_op jit(solution)/shard_map/pallas_call | solution.py:444
  48.3 2.1 %shard_map.86 = (bf16[128,256]{1,0:T(8,128)(2,1)}, bf16[128,768]{1,0:T(8,128)(2,1)}, f32[768,256]{1,0:T(8,128)}) custom-call(bf16[128,256]{1,0:T(8,128)(2,1)} %get-tuple-element.6.hidden_in, bf16[128,768]{1,0:T(8,128)(2,1)} %get-tuple-element.7.xgrad_in, bf16[2,2,1,384,128]{4,3,2,1,0:T(8,128)(2,1)} %bitcast.2), custom_call_target="tpu_custom_call" | custom-call | tf_op jit(solution)/shard_map/pallas_call | solution.py:466

commit v8 on v7

--- a/solution.py
+++ b/solution.py
@@ -218,32 +218,29 @@
     def features_arrive():
         arrive(feat_all.at[:, pl.ds(0, (n_blk - 1) * tile)], fe_s.at[0], fe_r.at[0])
 
-    def terms_start():
-        for h in range(2):
-            arrive(pair_in.at[h], pp_s.at[h], pp_r.at[h])
-            both16[h] = (pg_part[h] + pair_in[h].astype(F32)).astype(BF16)
-        for h in range(2):
-            term = dot(feat_all[...], both16[h])
-            dw_sum[h, 0:fhalf, :] = term
-            dw16[h, 0:fhalf, :] = term.astype(BF16)
-            if n_chip * r1 > fhalf and not direct:
-                rest = jnp.zeros((n_chip * r1 - fhalf, half), F32)
-                dw_sum[h, fhalf:, :] = rest
-                dw16[h, fhalf:, :] = rest.astype(BF16)
+    def terms_start(h):
+        arrive(pair_in.at[h], pp_s.at[h], pp_r.at[h])
+        both16[h] = (pg_part[h] + pair_in[h].astype(F32)).astype(BF16)
+        term = dot(feat_all[...], both16[h])
+        dw_sum[h, 0:fhalf, :] = term
+        dw16[h, 0:fhalf, :] = term.astype(BF16)
         if direct:
             for to, to_col, _, _ in others:
                 owner = to * n_col + to_col
                 send(
-                    dw16.at[:, rows(owner, r1)], dw_in.at[:, rows(mine, r1)],
-                    dc_s.at[0, 0], dc_r.at[0, 0], 2 * to + core, to_col, owner < n_own, keep=False,
+                    dw16.at[h, rows(owner, r1)], dw_in.at[h, rows(mine, r1)],
+                    dc_s.at[h, 0], dc_r.at[h, 0], 2 * to + core, to_col, owner < n_own, keep=False,
                 )
             return
-        for h in range(2):
-            for k, to, _ in chips:
-                send(
-                    dw16.at[h, rows(to, r1)], dw_in.at[h, rows(chip, r1)],
-                    dc_s.at[h, k], dc_r.at[h, chip], 2 * to + core, c,
-                )
+        if n_chip * r1 > fhalf:
+            rest = jnp.zeros((n_chip * r1 - fhalf, half), F32)
+            dw_sum[h, fhalf:, :] = rest
+            dw16[h, fhalf:, :] = rest.astype(BF16)
+        for k, to, _ in chips:
+            send(
+                dw16.at[h, rows(to, r1)], dw_in.at[h, rows(chip, r1)],
+                dc_s.at[h, k], dc_r.at[h, chip], 2 * to + core, c,
+            )
 
     def owners_start():
         for k, to, _ in chips:
@@ -252,34 +249,35 @@
                 pc_s.at[0, 0], pc_r.at[0, 0], 2 * to + core, c, keep=False,
             )
 
-    def result_direct():
+    def result_direct(h):
         count = len(others) * r1
 
         @pl.when(mine < n_own)
         def _():
-            arrive(dw_in.at[:, pl.ds(0, count)], dc_s.at[0, 0], dc_r.at[0, 0])
-            piece = dw_sum[:, rows(mine, r1), :]
+            arrive(dw_in.at[h, pl.ds(0, count)], dc_s.at[h, 0], dc_r.at[h, 0])
+            piece = dw_sum[h, rows(mine, r1), :]
             for _, _, src, src_col in others:
-                piece = piece + dw_in[:, rows(src * n_col + src_col, r1), :].astype(F32)
-            dw_all[core, :, rows(mine, r1), :] = piece.astype(BF16)
-
-        at = dw_all.at[core, :, rows(mine, r1)]
+                piece = piece + dw_in[h, rows(src * n_col + src_col, r1), :].astype(F32)
+            dw_all[core, h, rows(mine, r1), :] = piece.astype(BF16)
+
+        at = dw_all.at[core, h, rows(mine, r1)]
         for to, to_col, _, _ in others:
             send(
-                at, at, dg_s.at[0, 0], dg_r.at[0, 0], 2 * to + core, to_col, mine < n_own,
+                at, at, dg_s.at[h, 0], dg_r.at[h, 0], 2 * to + core, to_col, mine < n_own,
                 keep=False,
             )
 
-    def pass_direct():
+    def pass_direct(h):
         for owns in range(2):
             rest = (n_own - owns) * r1
 
             @pl.when((mine < n_own) == bool(owns))
             def _():
-                sent(dw16.at[:, pl.ds(0, rest)], dc_s.at[0, 0])
-                arrive(dw_all.at[core, :, pl.ds(0, rest)], dg_s.at[0, 0], dg_r.at[0, 0])
-
-        send(dw_all.at[core], dw_all.at[core], di_s.at[0, 0], di_r.at[0, 0], sib, c)
+                sent(dw16.at[h, pl.ds(0, rest)], dc_s.at[h, 0])
+                arrive(dw_all.at[core, h, pl.ds(0, rest)], dg_s.at[h, 0], dg_r.at[h, 0])
+
+        at = dw_all.at[core, h]
+        send(at, at, di_s.at[h, 0], di_r.at[h, 0], sib, c)
 
     def result_start(h):
         piece = dw_sum[h, rows(chip, r1), :]
@@ -342,16 +340,19 @@
     pair_start(0)
     pair_start(1)
     features_arrive()
-    terms_start()
+    terms_start(0)
+    terms_start(1)
     owners_start()
     for h in range(2):
         sent(grads.at[h, pl.ds(0, (n_col - 1) * tile)], gc_s.at[h, 0])
-    sent(feat_all.at[:, pl.ds(0, (n_blk - 1) * tile)], fe_s.at[0])
     if direct:
-        result_direct()
+        result_direct(0)
+        result_direct(1)
         own_features()
-        pass_direct()
-        arrive(dw_all.at[1 - core], di_s.at[0, 0], di_r.at[0, 0])
+        pass_direct(0)
+        pass_direct(1)
+        for h in range(2):
+            arrive(dw_all.at[1 - core, h], di_s.at[h, 0], di_r.at[h, 0])
     else:
         result_start(0)
         result_start(1)
@@ -368,10 +369,12 @@
         )
     outs[2].start()
     sent(both16.at[:, pl.ds(0, (n_chip - 1) * tile)], pc_s.at[0, 0])
+    sent(feat_all.at[:, pl.ds(0, (n_blk - 1) * tile)], fe_s.at[0])
     if direct:
         @pl.when(mine < n_own)
         def _():
-            sent(dw_in.at[:, pl.ds(0, len(others) * r1)], dg_s.at[0, 0])
+            for h in range(2):
+                sent(dw_in.at[h, pl.ds(0, len(others) * r1)], dg_s.at[h, 0])
 
     for copy, only in sends:
         if only is None:

time: 50.6 us -> 47.2 us (0.933)
  Pallas kernels: 49.7 us -> 46.4 us
    pallas_call x1, Pallas kernels: 47.6 us -> 44.3 us  [per_device(): pl.pallas_call(functools.partial(kernel, (n_blk, n_col, tile, fin, hid, r...]
where the time goes in v8:
time: 47.2 us; the launch traced here: 47 us
  Pallas kernels  46.4 us (98%)
  between operations  0.64 us (1%)
    pallas_call x1, Pallas kernels, per_device(): pl.pallas_call(functools.partial(kernel, (n_blk, n_col, tile, fin, hid, r...  44.3 us
    pallas_call x1, Pallas kernels, per_device(): pl.pallas_call(functools.partial(finish, scale, r1), out_shape=(jax.Shape...  2.11 us

profile of v8, /device:TPU:1, one launch (start us, length us, event | category | flops | bytes accessed | tf_op | source)
XLA Modules:
  0.0 47.0 jit_solution(15896218382262527499)
XLA Ops:
  0.6 44.3 %shard_map.85 = (bf16[128,256]{1,0:T(8,128)(2,1)}, bf16[128,768]{1,0:T(8,128)(2,1)}, bf16[2,2,384,128]{3,2,1,0:T(8,128)(2,1)}) custom-call(bf16[128,768]{1,0:T(8,128)(2,1)} %feat_h.1, s32[1,128]{1,0:T(1,128)} %order_h.1, bf16[768,256]{1,0:T(8,128)(2,1)} %weight_h.1, bf16[128,256]{1,0:T(8,128)(2,1)} %cot_h.1, s32[2,24]{1,0:T(2,128)} %bitcast.3, ...), custom_call_target="tpu_custom_call" | custom-call | flops 402653184 | bytes 4194304 | tf_op jit(solution)/shard_map/pallas_call | solution.py:447
  44.9 2.1 %shard_map.86 = (bf16[128,256]{1,0:T(8,128)(2,1)}, bf16[128,768]{1,0:T(8,128)(2,1)}, f32[768,256]{1,0:T(8,128)}) custom-call(bf16[128,256]{1,0:T(8,128)(2,1)} %get-tuple-element.6.hidden_in, bf16[128,768]{1,0:T(8,128)(2,1)} %get-tuple-element.7.xgrad_in, bf16[2,2,1,384,128]{4,3,2,1,0:T(8,128)(2,1)} %bitcast.2), custom_call_target="tpu_custom_call" | custom-call | tf_op jit(solution)/shard_map/pallas_call | solution.py:469

commit v9 on v8

--- a/solution.py
+++ b/solution.py
@@ -23,9 +23,9 @@
     hidden_h, xgrad_h, wgrad_h,
     feat, order, weight, cot, tiles, hidden, xgrad,
     adj, adj_t, feat_t, feat_all, panels, part, part16, agg_in, grads, pg_part, pg16,
-    pair_in, both16, chip_in, dw_sum, dw16, dw_in, dw_mid, dw_mid16, dw_col, dw_all,
+    pair_in, both16, chip_in, dw_sum, dw16, dw_in, dw_mid, dw_mid16, dw_col, dw_all, relay_in, relay_out,
     in_sem, out_sem, ag_s, ag_r, rc_s, rc_r, gc_s, gc_r, pp_s, pp_r, pc_s, pc_r,
-    fe_s, fe_r, dc_s, dc_r, dz_s, dz_r, dg_s, dg_r, dh_s, dh_r, di_s, di_r,
+    fe_s, fe_r, dc_s, dc_r, dz_s, dz_r, dg_s, dg_r, dh_s, dh_r, di_s, di_r, rl_s, rl_r,
 ):
     n_blk, n_col, tile, fin, hid, r1, r2, direct = dims
     n_chip = n_blk // 2
@@ -68,6 +68,15 @@
 
     chips = [(k, (chip + k) % n_chip, (chip + n_chip - k) % n_chip) for k in range(1, n_chip)]
     cols = [(k, (c + k) % n_col, (c + n_col - k) % n_col) for k in range(1, n_col)]
+
+    line = n_col == 4
+    ends = c % 3 == 0
+    far = 3 * (c % 2)
+    if line:
+        for h in range(2):
+            @pl.when(ends)
+            def _():
+                agg_in[h, rows(3 - c), :] = jnp.zeros((tile, half), BF16)
 
     loads = []
     for i, (src, dst) in enumerate(
@@ -140,10 +149,16 @@
             return 0
 
         lax.fori_loop(0, n_col * tile // step, forward, 0)
+        if line:
+            send(
+                part16.at[h, rows(3 - c)], relay_in.at[h], rl_s.at[h, 0], rl_r.at[h],
+                b, 1 + c // 3, ends,
+            )
         for k, to, _ in cols:
-            send(
-                part16.at[h, rows(to)], agg_in.at[h, rows(c)], rc_s.at[h, 0], rc_r.at[h, 0], b, to,
-                keep=False,
+            only = {1: c != 3, 2: ends, 3: c != 0}[k] if line else None
+            send(
+                part16.at[h, rows(to)], agg_in.at[h, rows(c)], rc_s.at[h, k], rc_r.at[h, c], b, to,
+                only,
             )
 
     for k, to, _ in chips:
@@ -155,6 +170,19 @@
         keep=False,
     )
 
+    if line:
+        for h in range(2):
+            @pl.when(c % 3 != 0)
+            def _():
+                arrive(relay_in.at[h], rl_s.at[h, 0], rl_r.at[h])
+                both = part[h, rows(far), :] + relay_in[h].astype(F32)
+                relay_out[h] = both.astype(BF16)
+
+            send(
+                relay_out.at[h], agg_in.at[h, rows(c)], rl_s.at[h, 1], rc_r.at[h, c],
+                b, far, c % 3 != 0,
+            )
+
     def turn(g, _):
         for r in range(n_col):
             adj_t[rows(g), r * tile:(r + 1) * tile] = (
@@ -170,7 +198,12 @@
     root = 0.7978845608028654
     for h in range(2):
         agg = part[h, rows(c), :]
-        arrive(agg_in.at[h, pl.ds(0, (n_col - 1) * tile)], rc_s.at[h, 0], rc_r.at[h, 0])
+        for k, _, src in cols:
+            come = functools.partial(arrive, agg_in.at[h, rows(src)], rc_s.at[h, k], rc_r.at[h, src])
+            if line and k != 2:
+                pl.when(c != (3 if k == 3 else 0))(come)
+            else:
+                come()
         for k, _, src in cols:
             agg = agg + agg_in[h, rows(src), :].astype(F32)
         inner = root * (agg + 0.044715 * agg * agg * agg)
@@ -182,13 +215,13 @@
         grads[h, rows(c), :] = (cot[:, lanes].astype(F32) * slope).astype(BF16)
         at = grads.at[h, rows(c)]
         for k, to, _ in cols:
-            send(at, at, gc_s.at[h, 0], gc_r.at[h, 0], b, to, keep=False)
+            only = {1: c != 3, 2: None, 3: c != 0}[k] if line else None
+            send(at, at, gc_s.at[h, k], gc_r.at[h, c], b, to, only)
         hidden[:, lanes] = (0.5 * agg * (1.0 + th)).astype(BF16)
     outs = [pltpu.make_async_copy(hidden, hidden_h, out_sem.at[0])]
     outs[0].start()
     for h in range(2):
         sent(panels.at[h, pl.ds(0, (n_blk - 1) * tile)], ag_s.at[h, 0])
-        sent(part16.at[h, pl.ds(0, (n_col - 1) * tile)], rc_s.at[h, 0])
 
     bstep = 4 * tile if n_blk % 4 == 0 else tile
     others = [
@@ -198,7 +231,12 @@
     mine = chip * n_col + c
 
     def pair_start(h):
-        arrive(grads.at[h, pl.ds(0, (n_col - 1) * tile)], gc_s.at[h, 0], gc_r.at[h, 0])
+        for k, _, src in cols:
+            come = functools.partial(arrive, grads.at[h, rows(src)], gc_s.at[h, k], gc_r.at[h, src])
+            if line and k == 2:
+                pl.when(ends)(come)
+            else:
+                come()
 
         def backward(i, _):
             if turned:
@@ -337,14 +375,19 @@
         outs.append(pltpu.make_async_copy(xgrad, xgrad_h, out_sem.at[1]))
         outs[1].start()
 
+    if line:
+        for h in range(2):
+            at = grads.at[h, rows(far)]
+            pl.when(c % 3 != 0)(
+                functools.partial(arrive, at, gc_s.at[h, 0], gc_r.at[h, far])
+            )
+            send(at, at, gc_s.at[h, 0], gc_r.at[h, far], b, 3 - far, c % 3 != 0)
     pair_start(0)
     pair_start(1)
     features_arrive()
     terms_start(0)
     terms_start(1)
     owners_start()
-    for h in range(2):
-        sent(grads.at[h, pl.ds(0, (n_col - 1) * tile)], gc_s.at[h, 0])
     if direct:
         result_direct(0)
         result_direct(1)
@@ -433,12 +476,13 @@
         vmem((2, n_sum * r1, half), BF16),
         vmem((2, n_col * r2, half), F32), vmem((2, n_col * r2, half), BF16),
         vmem((2, n_col * r2, half), BF16), vmem((2, 2, fhalf, half) if direct else (2, 2, n_chip, n_col * r2, half), BF16),
+        vmem((2, tile, half), BF16), vmem((2, tile, half), BF16),
         dma(5), dma(3), dma(2, 2 * n_chip), dma(2, n_blk),
         dma(2, n_col), dma(2, n_col), dma(2, n_col), dma(2, n_col),
         dma(2), dma(2), dma(2, n_chip), dma(2, n_chip),
         dma(2 * n_chip), dma(n_blk), dma(2, n_sum), dma(2, n_sum),
         dma(2, n_col), dma(2, n_col), dma(2, n_sum + n_col), dma(2, n_sum + n_col),
-        dma(2, n_chip), dma(2, n_chip), dma(2, n_sum), dma(2, n_sum),
+        dma(2, n_chip), dma(2, n_chip), dma(2, n_sum), dma(2, n_sum), dma(2, 2), dma(2),
     ]
     far = pl.BlockSpec(memory_space=pltpu.HBM)
     free = pl.BlockSpec(memory_space=pl.ANY)

time: 47.2 us -> 49.5 us (1.049)
  Pallas kernels: 46.4 us -> 48.7 us
    pallas_call x1, Pallas kernels: 44.3 us -> 46.6 us  [per_device(): pl.pallas_call(functools.partial(kernel, (n_blk, n_col, tile, fin, hid, r...]
where the time goes in v9:
time: 49.5 us; the launch traced here: 49.4 us
  Pallas kernels  48.7 us (98%)
  between operations  0.64 us (1%)
    pallas_call x1, Pallas kernels, per_device(): pl.pallas_call(functools.partial(kernel, (n_blk, n_col, tile, fin, hid, r...  46.6 us
    pallas_call x1, Pallas kernels, per_device(): pl.pallas_call(functools.partial(finish, scale, r1), out_shape=(jax.Shape...  2.11 us

profile of v9, /device:TPU:1, one launch (start us, length us, event | category | flops | bytes accessed | tf_op | source)
XLA Modules:
  0.0 49.4 jit_solution(4489488080089438176)
XLA Ops:
  0.6 46.6 %shard_map.85 = (bf16[128,256]{1,0:T(8,128)(2,1)}, bf16[128,768]{1,0:T(8,128)(2,1)}, bf16[2,2,384,128]{3,2,1,0:T(8,128)(2,1)}) custom-call(bf16[128,768]{1,0:T(8,128)(2,1)} %feat_h.1, s32[1,128]{1,0:T(1,128)} %order_h.1, bf16[768,256]{1,0:T(8,128)(2,1)} %weight_h.1, bf16[128,256]{1,0:T(8,128)(2,1)} %cot_h.1, s32[2,24]{1,0:T(2,128)} %bitcast.3, ...), custom_call_target="tpu_custom_call" | custom-call | flops 402653184 | bytes 4194304 | tf_op jit(solution)/shard_map/pallas_call | solution.py:491
  47.2 2.1 %shard_map.86 = (bf16[128,256]{1,0:T(8,128)(2,1)}, bf16[128,768]{1,0:T(8,128)(2,1)}, f32[768,256]{1,0:T(8,128)}) custom-call(bf16[128,256]{1,0:T(8,128)(2,1)} %get-tuple-element.6.hidden_in, bf16[128,768]{1,0:T(8,128)(2,1)} %get-tuple-element.7.xgrad_in, bf16[2,2,1,384,128]{4,3,2,1,0:T(8,128)(2,1)} %bitcast.2), custom_call_target="tpu_custom_call" | custom-call | tf_op jit(solution)/shard_map/pallas_call | solution.py:513

commit v10 on v5

--- a/solution.py
+++ b/solution.py
@@ -335,13 +335,13 @@
     features_arrive()
     terms_start(0)
     terms_start(1)
+    result_start(0)
     owners_start(0)
     owners_start(1)
-    result_start(0)
     result_start(1)
-    own_features()
     result_pass(0)
     result_pass(1)
+    own_features()
     result_arrive(0)
     result_arrive(1)
     if direct:

time: 47.2 us -> 47.1 us (level)
  no operation moved by 1% of the time
where the time goes in v10:
time: 47.1 us; the launch traced here: 46.9 us
  Pallas kernels  46.3 us (98%)
  between operations  0.64 us (1%)
    pallas_call x1, Pallas kernels, per_device(): pl.pallas_call(functools.partial(kernel, (n_blk, n_col, tile, fin, hid, r...  44.2 us
    pallas_call x1, Pallas kernels, per_device(): pl.pallas_call(functools.partial(finish, scale, r1), out_shape=(jax.Shape...  2.11 us

profile of v10, /device:TPU:1, one launch (start us, length us, event | category | flops | bytes accessed | tf_op | source)
XLA Modules:
  0.0 46.9 jit_solution(15440674504229314595)
XLA Ops:
  0.6 44.2 %shard_map.85 = (bf16[128,256]{1,0:T(8,128)(2,1)}, bf16[128,768]{1,0:T(8,128)(2,1)}, bf16[2,2,384,128]{3,2,1,0:T(8,128)(2,1)}) custom-call(bf16[128,768]{1,0:T(8,128)(2,1)} %feat_h.1, s32[1,128]{1,0:T(1,128)} %order_h.1, bf16[768,256]{1,0:T(8,128)(2,1)} %weight_h.1, bf16[128,256]{1,0:T(8,128)(2,1)} %cot_h.1, s32[2,24]{1,0:T(2,128)} %bitcast.3, ...), custom_call_target="tpu_custom_call" | custom-call | flops 402653184 | bytes 4194304 | tf_op jit(solution)/shard_map/pallas_call | solution.py:422
  44.8 2.1 %shard_map.86 = (bf16[128,256]{1,0:T(8,128)(2,1)}, bf16[128,768]{1,0:T(8,128)(2,1)}, f32[768,256]{1,0:T(8,128)}) custom-call(bf16[128,256]{1,0:T(8,128)(2,1)} %get-tuple-element.6.hidden_in, bf16[128,768]{1,0:T(8,128)(2,1)} %get-tuple-element.7.xgrad_in, bf16[2,2,1,384,128]{4,3,2,1,0:T(8,128)(2,1)} %bitcast.2), custom_call_target="tpu_custom_call" | custom-call | tf_op jit(solution)/shard_map/pallas_call | solution.py:444
